TPU v7x, 128 devices: a whole 4x4x4 slice. The times are simulated.
128 devices in a mesh: img: 16 (over y, z_lo, core), patch: 8 (over z_hi, x).
Axes of the slice: x: 4, y: 4, z: 4 (z_hi: 2, z_lo: 2; z = z_hi * 2 + z_lo), core: 2. Of those that a mesh axis runs over, the one named last changes fastest.
Arguments:
- latents_now: bfloat16 [16, 2048, 1280], P('img', 'patch'), may hold values from -6 to 6
- latents_stale: bfloat16 [16, 2048, 1280], P('img', 'patch'), may hold values from -6 to 6
- w_query: bfloat16 [1280, 640], replicated, may hold values from -1 to 1
- w_key: bfloat16 [1280, 640], replicated, may hold values from -1 to 1
- w_value: bfloat16 [1280, 640], replicated, may hold values from -0.15625 to 0.15625
- w_out: bfloat16 [640, 1280], replicated, may hold values from -1.5 to 1.5
- cotangent: bfloat16 [16, 2048, 1280], P('img', 'patch'), may hold values from -6 to 6
Outputs:
- mixed: bfloat16 [16, 2048, 1280], P('img', 'patch')
- grad_latents: bfloat16 [16, 2048, 1280], P('img', 'patch')
- grad_value: float32 [1280, 640], P('patch')
- grad_out: float32 [640, 1280], P('patch')
All inputs are finite; a program needn't handle non-finite values.
Results may differ from a plain program's by a relative error of at most 0.029.
Values may be sent and summed in bfloat16 or wider, within the bound.
A program may use at most 192 MiB of HBM per device.

v0:
```python
import jax
import jax.numpy as jnp
from jax import lax
from jax.sharding import PartitionSpec as P

HEADS = 10
HEAD_DIM = 64


def project(a, w):
    return jnp.dot(a, w, preferred_element_type=jnp.float32).astype(jnp.bfloat16)


def split_heads(a, heads):
    return a.reshape(a.shape[0], heads, a.shape[1] // heads)


def on_device(latents_now, latents_stale, w_query, w_key, w_value, w_out, cotangent):
    scale = HEAD_DIM ** (-0.5)
    x_rows = latents_now[0]
    stale_rows = latents_stale[0]
    grad_rows = cotangent[0]
    tok_rows = x_rows.shape[0]
    start = lax.axis_index("patch") * tok_rows
    query = project(x_rows, w_query)
    key_new = project(x_rows, w_key)
    value_new = project(x_rows, w_value)
    key_old = project(stale_rows, w_key)
    value_old = project(stale_rows, w_value)
    key_all_old, value_all_old = (
        lax.all_gather(key_old, "patch", axis=0, tiled=True),
        lax.all_gather(value_old, "patch", axis=0, tiled=True),
    )
    key_mix = lax.dynamic_update_slice_in_dim(key_all_old, key_new, start, 0)
    value_mix = lax.dynamic_update_slice_in_dim(value_all_old, value_new, start, 0)
    qh = split_heads(query, HEADS)
    scores = (
        jnp.einsum(
            "qhd,khd->hqk", qh, split_heads(key_mix, HEADS), preferred_element_type=jnp.float32
        )
        * scale
    )
    weights = jax.nn.softmax(scores, axis=-1).astype(jnp.bfloat16)
    att = jnp.einsum(
        "hqk,khd->qhd", weights, split_heads(value_mix, HEADS), preferred_element_type=jnp.float32
    )
    att = att.reshape(tok_rows, -1).astype(jnp.bfloat16)
    mixed = jnp.dot(att, w_out, preferred_element_type=jnp.float32)
    key_all, value_all = (
        lax.all_gather(key_new, "patch", axis=0, tiled=True),
        lax.all_gather(value_new, "patch", axis=0, tiled=True),
    )
    kh = split_heads(key_all, HEADS)
    vh = split_heads(value_all, HEADS)
    fresh = jnp.einsum("qhd,khd->hqk", qh, kh, preferred_element_type=jnp.float32) * scale
    prob = jax.nn.softmax(fresh, axis=-1)
    prob16 = prob.astype(jnp.bfloat16)
    attend = jnp.einsum("hqk,khd->qhd", prob16, vh, preferred_element_type=jnp.float32)
    attend = attend.reshape(tok_rows, -1).astype(jnp.bfloat16)
    dattend = jnp.dot(grad_rows, w_out.T, preferred_element_type=jnp.float32).astype(jnp.bfloat16)
    dah = split_heads(dattend, HEADS)
    dprob = jnp.einsum("qhd,khd->hqk", dah, vh, preferred_element_type=jnp.float32)
    delta = jnp.sum(
        dah.astype(jnp.float32) * split_heads(attend, HEADS).astype(jnp.float32), axis=-1
    ).T
    dscore = (prob * (dprob - delta[:, :, None]) * scale).astype(jnp.bfloat16)
    dquery = jnp.einsum("hqk,khd->qhd", dscore, kh, preferred_element_type=jnp.float32)
    dquery = dquery.reshape(tok_rows, -1).astype(jnp.bfloat16)
    dkey_part = jnp.einsum("hqk,qhd->khd", dscore, qh, preferred_element_type=jnp.float32)
    dvalue_part = jnp.einsum("hqk,qhd->khd", prob16, dah, preferred_element_type=jnp.float32)
    dkey_part = dkey_part.reshape(dkey_part.shape[0], -1).astype(jnp.bfloat16)
    dvalue_part = dvalue_part.reshape(dvalue_part.shape[0], -1).astype(jnp.bfloat16)
    dkey, dvalue = (
        lax.psum_scatter(dkey_part, "patch", scatter_dimension=0, tiled=True).astype(jnp.float32),
        lax.psum_scatter(dvalue_part, "patch", scatter_dimension=0, tiled=True).astype(jnp.float32),
    )
    dkey = dkey.astype(jnp.bfloat16)
    dvalue = dvalue.astype(jnp.bfloat16)
    grad_x = jnp.dot(dquery, w_query.T, preferred_element_type=jnp.float32)
    grad_x = grad_x + jnp.dot(dkey, w_key.T, preferred_element_type=jnp.float32)
    grad_x = grad_x + jnp.dot(dvalue, w_value.T, preferred_element_type=jnp.float32)
    grad_v = jnp.dot(x_rows.T, dvalue, preferred_element_type=jnp.float32)
    grad_o = jnp.dot(attend.T, grad_rows, preferred_element_type=jnp.float32)
    summed = (
        lax.psum(grad_v.astype(jnp.bfloat16), "img").astype(jnp.float32),
        lax.psum(grad_o.astype(jnp.bfloat16), "img").astype(jnp.float32),
    )
    grad_value, grad_out = (
        lax.psum_scatter(
            summed[0].astype(jnp.bfloat16), "patch", scatter_dimension=0, tiled=True
        ).astype(jnp.float32),
        lax.psum_scatter(
            summed[1].astype(jnp.bfloat16), "patch", scatter_dimension=0, tiled=True
        ).astype(jnp.float32),
    )
    return (
        mixed.astype(jnp.bfloat16)[None],
        grad_x.astype(jnp.bfloat16)[None],
        grad_value,
        grad_out,
    )


def solution(mesh):
    placed = (
        P("img", "patch", None),
        P("img", "patch", None),
        P(),
        P(),
        P(),
        P(),
        P("img", "patch", None),
    )
    return jax.shard_map(
        on_device,
        mesh=mesh,
        in_specs=placed,
        out_specs=(
            P("img", "patch", None),
            P("img", "patch", None),
            P("patch", None),
            P("patch", None),
        ),
        check_vma=False,
    )
```

profile of v0, /device:TPU:1, one launch (start us, length us, event | category | flops | bytes accessed | tf_op | source)
XLA Modules:
  0.0 693.8 jit_solution(17875584363935897731)
XLA Ops:
  7.2 1.4 copy-done
  8.6 2.5 convolution_convert_fusion.9
  11.1 0.0 all-gather.9.cloned.1.call-start
  11.2 61.5 %all-gather.7.cloned.1.call-done = bf16[2048,640]{1,0:T(8,128)(2,1)} async-done(((bf16[256,640]{1,0:T(8,128)(2,1)}), bf16[2048,640]{1,0:T(8,128)(2,1)}) %all-gather.7.cloned.1.call-update) | async-done | bytes 2621456 | tf_op jit(solution)/shard_map/all_gather | solution.py:31
  72.7 2.6 constant_dynamic-update-slice_fusion
  75.3 0.0 all-gather.5.cloned.1.call-start
  75.4 2.5 convolution_convert_fusion.12
  77.9 0.0 reduce-scatter.9.cloned.1.call-start
  78.0 3.0 convolution_convert_fusion.10
  81.0 1.9 copy.32
  82.9 3.1 convolution_convert_fusion.7
  86.0 1.9 copy.35
  87.9 45.2 %all-gather.9.cloned.1.call-done = bf16[2048,640]{1,0:T(8,128)(2,1)} async-done(((bf16[256,640]{1,0:T(8,128)(2,1)}), bf16[2048,640]{1,0:T(8,128)(2,1)}) %all-gather.9.cloned.1.call-update) | async-done | bytes 2621456 | tf_op jit(solution)/shard_map/all_gather | solution.py:50
  133.1 4.6 copy.34
  137.6 11.6 %fusion.32 = (f32[10,256]{1,0:T(8,128)S(1)}, f32[10,256,2048]{2,1,0:T(8,128)}) fusion(bf16[256,10,64]{0,2,1:T(8,128)(2,1)} %bitcast.99, bf16[2048,10,64]{0,2,1:T(8,128)(2,1)} %bitcast.90), kind=kOutput, calls=%fused_computation.51 | convolution fusion | flops 686819328 | bytes 23930880 | tf_op jit(solution)/shard_map/sub | solution.py:56
  149.3 8.9 %fusion.11 = bf16[10,256,2048]{2,1,0:T(8,128)(2,1)S(1)} fusion(f32[10,256,2048]{2,1,0:T(8,128)} %get-tuple-element.25, f32[10,256]{1,0:T(8,128)S(1)} %get-tuple-element.24), kind=kLoop, calls=%fused_computation.14 | loop fusion | flops 10485760 | bytes 31467520 | tf_op jit(solution)/shard_map/convert_element_type | solution.py:57
  158.2 3.9 convolution_convert_fusion.2
  162.1 0.7 copy-done.1
  162.8 0.0 all-gather.11.cloned.1.call-start
  162.9 30.6 %all-gather.5.cloned.1.call-done = bf16[2048,640]{1,0:T(8,128)(2,1)} async-done(((bf16[256,640]{1,0:T(8,128)(2,1)}), bf16[2048,640]{1,0:T(8,128)(2,1)}) %all-gather.5.cloned.1.call-update) | async-done | bytes 2621456 | tf_op jit(solution)/shard_map/all_gather | solution.py:32
  193.5 2.6 constant_dynamic-update-slice_fusion.1
  196.2 77.0 %reduce-scatter.9.cloned.1.call-done = bf16[256,640]{0,1:T(8,128)(2,1)} async-done(((bf16[2048,640]{0,1:T(8,128)(2,1)}), bf16[256,640]{0,1:T(8,128)(2,1)}) %reduce-scatter.9.cloned.1.call-update) | async-done | bytes 327696 | tf_op jit(solution)/shard_map/reduce_scatter | solution.py:75
  273.2 2.9 fusion.12
  276.1 3.5 copy.38
  279.7 0.2 reduce-scatter.11.cloned.1.call-start
  279.9 54.3 %all-gather.11.cloned.1.call-done = bf16[2048,640]{1,0:T(8,128)(2,1)} async-done(((bf16[256,640]{1,0:T(8,128)(2,1)}), bf16[2048,640]{1,0:T(8,128)(2,1)}) %all-gather.11.cloned.1.call-update) | async-done | bytes 2621456 | tf_op jit(solution)/shard_map/all_gather | solution.py:51
  334.2 4.5 copy.36
  338.7 8.1 %multiply_reduce_fusion.2 = (f32[256,10]{0,1:T(8,128)S(1)}, bf16[10,64,256]{2,1,0:T(8,128)(2,1)S(1)}) fusion(bf16[256,10,64]{0,2,1:T(8,128)(2,1)} %bitcast.94, bf16[2048,10,64]{0,2,1:T(8,128)(2,1)} %bitcast.92, bf16[10,256,2048]{2,1,0:T(8,128)(2,1)} %copy-done.1), kind=kOutput, calls=%fused_computation.45 | convolution fusion | flops 671905280 | bytes 13772800 | tf_op jit(solution)/shard_map/hqk,khd->qhd/dot_general | solution.py:58
  346.8 1.8 convolution_convert_fusion
  348.7 12.4 %multiply_convert_fusion = bf16[10,256,2048]{2,1,0:T(8,128)(2,1)} fusion(f32[10,256]{1,0:T(8,128)S(1)} %bitcast.105, f32[10,256,2048]{2,1,0:T(8,128)} %get-tuple-element.25, f32[10,256]{1,0:T(8,128)S(1)} %get-tuple-element.24, bf16[256,10,64]{0,2,1:T(8,128)(2,1)} %bitcast.95, bf16[2048,10,64]{0,2,1:T(8,128)(2,1)} %bitcast.93), kind=kOutput, calls=%fused_computation.2 | convolution fusion | flops 697303040 | bytes 34426880 | tf_op jit(solution)/shard_map/qhd,khd->hqk/dot_general | solution.py:62
  361.0 7.5 %convolution_convert_fusion.3 = bf16[10,64,2048]{2,1,0:T(8,128)(2,1)} fusion(bf16[256,10,64]{0,2,1:T(8,128)(2,1)S(1)} %bitcast.101, bf16[10,256,2048]{2,1,0:T(8,128)(2,1)} %multiply_convert_fusion), kind=kOutput, calls=%fused_computation.18 | convolution fusion | flops 672399360 | bytes 13434880 | tf_op jit(solution)/shard_map/hqk,qhd->khd/dot_general | solution.py:69
  368.5 0.3 all-reduce.3.cloned.1.call-start
  368.8 4.5 copy.31
  373.3 4.5 copy.33
  377.8 11.5 %fusion.31 = (f32[10,256]{1,0:T(8,128)S(1)}, f32[10,256,2048]{2,1,0:T(8,128)}) fusion(bf16[256,10,64]{0,2,1:T(8,128)(2,1)} %bitcast.100, bf16[2048,10,64]{0,2,1:T(8,128)(2,1)} %bitcast.98), kind=kOutput, calls=%fused_computation.50 | convolution fusion | flops 686819328 | bytes 23930880 | tf_op jit(solution)/shard_map/sub | solution.py:43
  389.2 11.2 %fusion.20 = bf16[10,64,256]{2,1,0:T(8,128)(2,1)S(1)} fusion(bf16[2048,10,64]{0,2,1:T(8,128)(2,1)} %bitcast.97, f32[10,256,2048]{2,1,0:T(8,128)} %get-tuple-element.23, f32[10,256]{1,0:T(8,128)S(1)} %get-tuple-element.22), kind=kOutput, calls=%fused_computation.36 | convolution fusion | flops 681738240 | bytes 23930880 | tf_op jit(solution)/shard_map/hqk,khd->qhd/dot_general | solution.py:44
  400.5 1.5 fusion.14
  402.0 0.3 copy-done.2
  402.4 7.5 %convolution_convert_fusion.5 = bf16[10,64,256]{2,1,0:T(8,128)(2,1)S(1)} fusion(bf16[2048,10,64]{0,2,1:T(8,128)(2,1)S(1)} %bitcast.91, bf16[10,256,2048]{2,1,0:T(8,128)(2,1)} %multiply_convert_fusion), kind=kOutput, calls=%fused_computation.28 | convolution fusion | flops 671252480 | bytes 13434880 | tf_op jit(solution)/shard_map/hqk,khd->qhd/dot_general | solution.py:67
  409.9 1.8 fusion.33
  411.7 1.8 copy.39
  413.5 74.1 %reduce-scatter.11.cloned.1.call-done = bf16[80,1280]{1,0:T(8,128)(2,1)} async-done(((bf16[640,1280]{1,0:T(8,128)(2,1)}), bf16[80,1280]{1,0:T(8,128)(2,1)}) %reduce-scatter.11.cloned.1.call-update) | async-done | bytes 204816 | tf_op jit(solution)/shard_map/reduce_scatter | solution.py:92
  487.7 80.0 %reduce-scatter.7.cloned.1.call-done = bf16[256,640]{0,1:T(8,128)(2,1)} async-done(((bf16[2048,640]{0,1:T(8,128)(2,1)}), bf16[256,640]{0,1:T(8,128)(2,1)}) %reduce-scatter.7.cloned.1.call-update) | async-done | bytes 327696 | tf_op jit(solution)/shard_map/reduce_scatter | solution.py:74
  567.7 2.2 convolution_add_fusion.1
  569.9 1.6 fusion.15
  571.5 112.2 %all-reduce.3.cloned.1.call-done = (bf16[160,640]{0,1:T(8,128)(2,1)}, bf16[80,1280]{1,0:T(8,128)(2,1)}) async-done(((bf16[160,640]{0,1:T(8,128)(2,1)}, bf16[80,1280]{1,0:T(8,128)(2,1)}), (bf16[160,640]{0,1:T(8,128)(2,1)}, bf16[80,1280]{1,0:T(8,128)(2,1)})) %all-reduce.3.cloned.1.call-update) | async-done | bytes 409616 | tf_op jit(solution)/shard_map/psum | solution.py:85
  683.7 1.9 copy.37
  685.6 1.7 convert_element_type.140
  (30 shorter events, 0.3 us)
Async XLA Ops:
  7.2 1.4 copy-start
  7.2 68.2 %copy-start.3 = (bf16[1280,640]{1,0:T(8,128)(2,1)S(1)}, bf16[1280,640]{1,0:T(8,128)(2,1)}, u32[]{:S(2)}) copy-start(bf16[1280,640]{1,0:T(8,128)(2,1)} %param.11) | copy-start | bytes 4915204
  7.2 65.5 %all-gather.7.cloned.1.call-start = ((), (), s32[]{:S(2)}) async-start(), calls=%async_computation.5 | async-start | bytes 2949120 | tf_op jit(solution)/shard_map/all_gather | solution.py:31
  11.1 122.0 %all-gather.9.cloned.1.call-start = ((), (), s32[]{:S(2)}) async-start(), calls=%async_computation.6 | async-start | bytes 2949120 | tf_op jit(solution)/shard_map/all_gather | solution.py:50
  75.3 118.2 %all-gather.5.cloned.1.call-start = ((), (), s32[]{:S(2)}) async-start(), calls=%async_computation.4 | async-start | bytes 2949120 | tf_op jit(solution)/shard_map/all_gather | solution.py:32
  77.9 195.3 %reduce-scatter.9.cloned.1.call-start = ((), (), s32[]{:S(2)}) async-start(), calls=%async_computation.9 | async-start | bytes 2949120 | tf_op jit(solution)/shard_map/reduce_scatter | solution.py:75
  149.3 8.9 %copy-start.4 = (bf16[256,640]{0,1:T(8,128)(2,1)S(1)}, bf16[256,640]{0,1:T(8,128)(2,1)}, u32[]{:S(2)}) copy-start(bf16[256,640]{0,1:T(8,128)(2,1)} %copy.35) | copy-start | bytes 983044
  158.1 4.7 copy-start.1
  162.8 171.3 %all-gather.11.cloned.1.call-start = ((), (), s32[]{:S(2)}) async-start(), calls=%async_computation.7 | async-start | bytes 2949120 | tf_op jit(solution)/shard_map/all_gather | solution.py:51
  196.2 215.5 %reduce-scatter.13.cloned.1.call-start = ((), (), s32[]{:S(2)}) async-start(), calls=%async_computation.11 | async-start | bytes 1843200
  279.7 208.0 %reduce-scatter.11.cloned.1.call-start = ((), (), s32[]{:S(2)}) async-start(), calls=%async_computation.10 | async-start | bytes 1843200 | tf_op jit(solution)/shard_map/reduce_scatter | solution.py:92
  338.7 8.1 %copy-start.9 = (bf16[1,256,1280]{2,1,0:T(8,128)(2,1)S(1)}, bf16[1,256,1280]{2,1,0:T(8,128)(2,1)}, u32[]{:S(2)}) copy-start(bf16[1,256,1280]{2,1,0:T(8,128)(2,1)} %param.13) | copy-start | bytes 1966084
  348.6 219.1 %reduce-scatter.7.cloned.1.call-start = ((), (), s32[]{:S(2)}) async-start(), calls=%async_computation.8 | async-start | bytes 2949120 | tf_op jit(solution)/shard_map/reduce_scatter | solution.py:74
  348.6 12.4 %copy-start.5 = (bf16[256,640]{0,1:T(8,128)(2,1)S(1)}, bf16[256,640]{0,1:T(8,128)(2,1)}, u32[]{:S(2)}) copy-start(bf16[256,640]{0,1:T(8,128)(2,1)} %copy.32) | copy-start | bytes 983044
  368.5 315.2 %all-reduce.3.cloned.1.call-start = ((), (), s32[]{:S(2)}) async-start(), calls=%async_computation.12 | async-start | bytes 1064960 | tf_op jit(solution)/shard_map/psum | solution.py:85
  389.2 11.3 %copy-start.6 = (bf16[640,1280]{1,0:T(8,128)(2,1)S(1)}, bf16[640,1280]{1,0:T(8,128)(2,1)}, u32[]{:S(2)}) copy-start(bf16[640,1280]{1,0:T(8,128)(2,1)} %param.12) | copy-start | bytes 4915204
  400.5 1.9 copy-start.2
  402.3 7.5 %copy-start.7 = (bf16[1280,640]{1,0:T(8,128)(2,1)S(1)}, bf16[1280,640]{1,0:T(8,128)(2,1)}, u32[]{:S(2)}) copy-start(bf16[1280,640]{1,0:T(8,128)(2,1)} %param.9) | copy-start | bytes 4915204
  567.7 2.2 copy-start.8
Sparse Core Ops, SparseCore 0:
  11.2 61.3 all-gather.6
  75.6 57.4 all-gather.8
  136.0 57.4 all-gather.4
  197.2 75.9 reduce-scatter.8
  275.9 58.2 all-gather.10
  337.8 72.7 reduce-scatter.12
  414.4 73.2 reduce-scatter.10
  491.5 76.1 reduce-scatter.6
  570.8 112.8 all-reduce.2
where the time goes:
time: 695 us; the launch traced here: 694 us
  waiting for transfers between devices  535 us (77%)
  matrix products  102 us (15%)
  local copies, waits for them, and re-layouts  31.4 us (5%)
  between operations  14 us (2%)
  other arithmetic  10.6 us (2%)
    psum x1, waiting for transfers between devices, on_device(): lax.psum(grad_v.astype(jnp.bfloat16), 'img').astype(jnp.float32)  112 us
    reduce_scatter x1, waiting for transfers between devices, on_device(): lax.psum_scatter(dkey_part, 'patch', scatter_dimension=0, tiled=True)  80 us
    reduce_scatter x1, waiting for transfers between devices, on_device(): lax.psum_scatter(dvalue_part, 'patch', scatter_dimension=0, tiled=True)  77 us
    reduce_scatter x1, waiting for transfers between devices, on_device(): lax.psum_scatter(summed[1].astype(jnp.bfloat16), 'patch', scatter_dimensi...  74.1 us
    all_gather x1, waiting for transfers between devices, on_device(): lax.all_gather(key_old, 'patch', axis=0, tiled=True)  61.5 us
    all_gather x1, waiting for transfers between devices, on_device(): lax.all_gather(value_new, 'patch', axis=0, tiled=True)  54.3 us
    all_gather x1, waiting for transfers between devices, on_device(): lax.all_gather(key_new, 'patch', axis=0, tiled=True)  45.2 us
    all_gather x1, waiting for transfers between devices, on_device(): lax.all_gather(value_old, 'patch', axis=0, tiled=True)  30.6 us
  transfers between devices with their start and end apart: 9, of which 8 were waited for; matrix products, arithmetic and copies ran while one was open for 19% of the time, Pallas kernels for 0%

commit v1 on v0

v1 whole, which is shorter than its diff:
```python
import jax
import jax.numpy as jnp
from jax import lax
from jax.experimental import pallas as pl
from jax.experimental.pallas import tpu as pltpu
from jax.sharding import PartitionSpec as P

HEADS = 10
HEAD_DIM = 64
N_PATCH = 8
N_IMG = 16
ROWS = 256
TOKENS = 2048
C = 1280
INNER = 640
PART = 832
SLOT = 208
HALF = 112
BF = jnp.bfloat16
F32 = jnp.float32
MESH = pl.DeviceIdType.MESH
NT = (((1,), (1,)), ((), ()))
NN = (((1,), (0,)), ((), ()))
SCALE = HEAD_DIM**-0.5
EXP2_SCALE = SCALE * 1.4426950408889634


def dot(a, b, dims=NN):
    return lax.dot_general(a, b, dims, preferred_element_type=F32)


def left_half(rows):
    return lax.broadcasted_iota(jnp.int32, (rows, 128), 1) < HEAD_DIM


def pair(a, b):
    return jnp.concatenate([a, b], axis=1)


def fresh_tile(qd, kv, acc_k, acc_v):
    left = left_half(ROWS)
    zero = jnp.zeros_like(qd)
    scores = dot(jnp.where(left, qd, zero), kv, NT)
    top = jnp.max(scores, axis=1, keepdims=True)
    e = jnp.exp2((scores - top) * EXP2_SCALE)
    inv = 1.0 / jnp.sum(e, axis=1, keepdims=True)
    e16 = e.astype(BF)
    a16 = (dot(e16, kv) * inv).astype(BF)
    delta = jnp.sum(
        jnp.where(left, 0.0, a16.astype(F32) * qd.astype(F32)), axis=1, keepdims=True
    )
    dprob = dot(jnp.where(left, zero, qd), kv, NT)
    ds = (e * (dprob - delta)).astype(BF)
    dq = dot(ds, kv) * (inv * SCALE)
    scaled = (qd.astype(F32) * jnp.where(left, inv * SCALE, inv)).T.astype(BF)
    acc_k[...] += dot(scaled[:HEAD_DIM], ds)
    acc_v[...] += dot(scaled[HEAD_DIM:], e16)
    return jnp.where(left, dq.astype(BF), a16)


def stale_tile(qd, kv):
    left = left_half(ROWS)
    scores = dot(jnp.where(left, qd, jnp.zeros_like(qd)), kv, NT)
    top = jnp.max(scores, axis=1, keepdims=True)
    e = jnp.exp2((scores - top) * EXP2_SCALE)
    inv = 1.0 / jnp.sum(e, axis=1, keepdims=True)
    out = (dot(e.astype(BF), kv) * inv).astype(BF)
    return pair(out[: ROWS // 2, HEAD_DIM:], out[ROWS // 2 :, HEAD_DIM:])


def kernel(
    x_hbm, s_hbm, wq_hbm, wk_hbm, wv_hbm, wo_hbm, g_hbm,
    mixed_ref, gradx_ref, gv_ref, go_ref,
    x, s, wq, wk, wv, wo, g, load_sem,
    st_kv, st_qd, st_ks, kv_w, qd_w, ks_w, kv_q, qd_q, ks_q,
    send_w, recv_w, send_q, recv_q, local_sem,
    acc_k, acc_v, kmix, out_w, out_q, dkv_w, dkv_q, att_w, att_q,
    home_a, home_d, home_p, home_t,
    rsend, rrecv, psend, precv,
    grads, from_core, from_y, ysum, from_xz, gathered, final,
    csem, ysend, yrecv, xsend, xrecv, gsend, grecv,
):
    img = lax.axis_index("img")
    me = lax.axis_index("patch")
    core = lax.rem(img, 2)
    zlo = lax.rem(img // 2, 2)
    yy = img // 4
    mine_e = me // 4
    first_q = 2 * lax.rem(me, 4)

    loads = []
    for n, (src, dst) in enumerate(
        ((x_hbm, x), (wk_hbm, wk), (wv_hbm, wv), (wq_hbm, wq), (g_hbm, g), (wo_hbm, wo), (s_hbm, s))
    ):
        copy = pltpu.make_async_copy(src, dst, load_sem.at[n])
        copy.start()
        loads.append(copy)

    barrier = pltpu.get_barrier_semaphore()
    for off in range(1, N_PATCH):
        pl.semaphore_signal(
            barrier, inc=1, device_id=(img, lax.rem(me + off, N_PATCH)), device_id_type=MESH
        )
    for off in range(1, N_IMG):
        pl.semaphore_signal(
            barrier, inc=1, device_id=(lax.rem(img + off, N_IMG), me), device_id_type=MESH
        )
    for off in range(1, N_PATCH):
        pl.semaphore_signal(
            barrier, inc=1,
            device_id=(img + 2 - 4 * zlo, lax.rem(me + off, N_PATCH)), device_id_type=MESH,
        )

    def to_whole(kind, stage, land, peer):
        return pltpu.make_async_remote_copy(
            src_ref=stage.at[peer], dst_ref=land.at[me],
            send_sem=send_w.at[kind, peer], recv_sem=recv_w.at[kind, me],
            device_id=(img, peer), device_id_type=MESH,
        )

    def from_whole(kind, land, peer):
        return pltpu.make_async_remote_copy(
            src_ref=land.at[peer], dst_ref=land.at[peer],
            send_sem=send_w.at[kind, peer], recv_sem=recv_w.at[kind, peer],
            device_id=(img, peer), device_id_type=MESH,
        )

    def to_quarter(kind, stage, land, peer):
        return pltpu.make_async_remote_copy(
            src_ref=stage.at[N_PATCH + peer // 4], dst_ref=land.at[me],
            send_sem=send_q.at[kind, peer], recv_sem=recv_q.at[kind, me],
            device_id=(img, peer), device_id_type=MESH,
        )

    def from_quarter(kind, land, peer):
        return pltpu.make_async_remote_copy(
            src_ref=land.at[peer], dst_ref=land.at[peer],
            send_sem=send_q.at[kind, peer], recv_sem=recv_q.at[kind, peer],
            device_id=(img, peer), device_id_type=MESH,
        )

    def quarter_rows(e):
        peer = 4 * e + me // 2
        return peer, pltpu.make_async_remote_copy(
            src_ref=st_qd.at[N_PATCH + e], dst_ref=qd_q.at[lax.rem(me, 2)],
            send_sem=send_q.at[1, e], recv_sem=recv_q.at[1, lax.rem(me, 2)],
            device_id=(img, peer), device_id_type=MESH,
        )

    def quarter_rows_in(t):
        return first_q + t, pltpu.make_async_remote_copy(
            src_ref=qd_q.at[t], dst_ref=qd_q.at[t],
            send_sem=send_q.at[1, t], recv_sem=recv_q.at[1, t],
            device_id=(img, first_q + t), device_id_type=MESH,
        )

    def peers(fn):
        def step(off, carry):
            fn(lax.rem(me + off, N_PATCH))
            return carry

        lax.fori_loop(1, N_PATCH, step, 0)

    def stage_pairs(stage, a, b):
        for h in range(HEADS):
            cols = slice(h * HEAD_DIM, (h + 1) * HEAD_DIM)
            stage[h] = pair(a[:, cols], b[:, cols])

    loads[0].wait()
    loads[1].wait()
    key = dot(x[...], wk[...]).astype(BF)
    loads[2].wait()
    value = dot(x[...], wv[...]).astype(BF)
    stage_pairs(st_kv, key, value)
    pl.semaphore_wait(barrier, 2 * (N_PATCH - 1) + N_IMG - 1)
    peers(lambda peer: to_whole(0, st_kv, kv_w, peer).start())
    kv_w[me] = st_kv[me]
    loads[3].wait()
    query = dot(x[...], wq[...]).astype(BF)
    loads[4].wait()
    loads[5].wait()
    dattend = dot(g[...], wo[...], NT).astype(BF)
    stage_pairs(st_qd, query, dattend)
    peers(lambda peer: to_whole(1, st_qd, qd_w, peer).start())
    qd_w[me] = st_qd[me]
    peers(lambda peer: to_quarter(0, st_kv, kv_q, peer).start())
    kv_q[me] = st_kv[N_PATCH + mine_e]
    for e in range(2):
        peer, copy = quarter_rows(e)

        @pl.when(peer != me)
        def _():
            copy.start()

        @pl.when(peer == me)
        def _():
            qd_q[lax.rem(me, 2)] = st_qd[N_PATCH + e]

    loads[6].wait()
    key_old = dot(s[...], wk[...]).astype(BF)
    value_old = dot(s[...], wv[...]).astype(BF)
    stage_pairs(st_ks, key_old, value_old)
    peers(lambda peer: to_whole(2, st_ks, ks_w, peer).start())
    ks_w[me] = st_ks[me]
    peers(lambda peer: to_quarter(2, st_ks, ks_q, peer).start())
    ks_q[me] = st_ks[N_PATCH + mine_e]

    def go_home(kind, src, land, peer):
        return pltpu.make_async_remote_copy(
            src_ref=src.at[peer], dst_ref=land.at[me],
            send_sem=rsend.at[kind, peer], recv_sem=rrecv.at[kind, me],
            device_id=(img, peer), device_id_type=MESH,
        )

    def come_home(kind, land, peer):
        return pltpu.make_async_remote_copy(
            src_ref=land.at[peer], dst_ref=land.at[peer],
            send_sem=rsend.at[kind, peer], recv_sem=rrecv.at[kind, peer],
            device_id=(img, peer), device_id_type=MESH,
        )

    def go_home_rows(kind, src, land, t):
        peer = first_q + t
        return peer, pltpu.make_async_remote_copy(
            src_ref=src.at[t], dst_ref=land.at[N_PATCH + mine_e],
            send_sem=psend.at[kind, t], recv_sem=precv.at[kind, mine_e],
            device_id=(img, peer), device_id_type=MESH,
        )

    def come_home_rows(kind, land, e):
        peer = 4 * e + me // 2
        return peer, pltpu.make_async_remote_copy(
            src_ref=land.at[N_PATCH + e], dst_ref=land.at[N_PATCH + e],
            send_sem=psend.at[kind, e], recv_sem=precv.at[kind, e],
            device_id=(img, peer), device_id_type=MESH,
        )

    def clear():
        acc_k[...] = jnp.zeros_like(acc_k)
        acc_v[...] = jnp.zeros_like(acc_v)

    def pack_dkv(out):
        for j in range(N_PATCH):
            cols = slice(j * ROWS, (j + 1) * ROWS)
            out[j] = pair(acc_k[:, cols].T.astype(BF), acc_v[:, cols].T.astype(BF))

    peers(lambda peer: from_whole(0, kv_w, peer).wait_recv())
    peers(lambda peer: from_whole(1, qd_w, peer).wait_recv())
    clear()

    def fresh_step(i, carry):
        out_w[i] = fresh_tile(qd_w[i], kv_w[...].reshape(TOKENS, 128), acc_k, acc_v)

        @pl.when(i != me)
        def _():
            go_home(0, out_w, home_a, i).start()

        return carry

    lax.fori_loop(0, N_PATCH, fresh_step, 0)
    home_a[me] = out_w[me]
    pack_dkv(dkv_w)
    peers(lambda peer: go_home(1, dkv_w, home_d, peer).start())
    home_d[me] = dkv_w[me]

    peers(lambda peer: from_quarter(0, kv_q, peer).wait_recv())
    for t in range(2):
        peer, copy = quarter_rows_in(t)

        @pl.when(peer != me)
        def _():
            copy.wait_recv()

    clear()

    def fresh_quarter_step(t, carry):
        out_q[t] = fresh_tile(qd_q[t], kv_q[...].reshape(TOKENS, 128), acc_k, acc_v)
        return carry

    lax.fori_loop(0, 2, fresh_quarter_step, 0)
    pack_dkv(dkv_q)

    def send_rows(kind, src, land):
        for t in range(2):
            peer, copy = go_home_rows(kind, src, land, t)

            @pl.when(peer != me)
            def _():
                copy.start()

            @pl.when(peer == me)
            def _():
                land[N_PATCH + mine_e] = src[t]

    send_rows(0, out_q, home_a)
    peers(lambda peer: go_home(2, dkv_q, home_p, peer).start())
    home_p[me] = dkv_q[me]

    peers(lambda peer: from_whole(2, ks_w, peer).wait_recv())
    kmix[...] = ks_w[...]

    def stale_step(i, carry):
        kmix[i] = kv_w[i]
        att_w[i] = stale_tile(qd_w[i], kmix[...].reshape(TOKENS, 128))
        kmix[i] = ks_w[i]

        @pl.when(i != me)
        def _():
            go_home(3, att_w, home_t, i).start()

        return carry

    lax.fori_loop(0, N_PATCH, stale_step, 0)
    home_t[me] = att_w[me]

    def receive_rows(kind, land):
        for e in range(2):
            peer, copy = come_home_rows(kind, land, e)

            @pl.when(peer != me)
            def _():
                copy.wait_recv()

    peers(lambda peer: come_home(0, home_a, peer).wait_recv())
    peers(lambda peer: come_home(1, home_d, peer).wait_recv())
    peers(lambda peer: come_home(2, home_p, peer).wait_recv())
    receive_rows(0, home_a)
    for e in range(2):
        total = home_p[4 * e].astype(F32)
        for n in range(1, 4):
            total = total + home_p[4 * e + n].astype(F32)
        home_d[N_PATCH + e] = total.astype(BF)

    def gather_heads(src, lo):
        return jnp.concatenate([src[h][:, lo : lo + HEAD_DIM] for h in range(HEADS)], axis=1)

    attend_t = gather_heads(home_a, HEAD_DIM).T
    dvalue = gather_heads(home_d, HEAD_DIM)
    x_t = x[...].T
    for q in range(N_PATCH):
        part = dot(x_t[160 * q : 160 * q + 160], dvalue).astype(BF)
        for c in range(5):
            grads[0, q, 160 * c : 160 * c + 160] = part[:, 128 * c : 128 * c + 128]
        part = dot(attend_t[80 * q : 80 * q + 80], g[...]).astype(BF)
        for c in range(10):
            grads[1, q, 80 * c : 80 * c + 80] = part[:, 128 * c : 128 * c + 128]
        grads[:, q, 800:] = jnp.zeros((2, PART - 800, 128), BF)

    core_copy = pltpu.make_async_remote_copy(
        src_ref=grads.at[1 - core], dst_ref=from_core,
        send_sem=csem.at[0], recv_sem=csem.at[1],
        device_id=(img + 1 - 2 * core, me), device_id_type=MESH,
    )
    core_copy.start()

    peers(lambda peer: from_quarter(2, ks_q, peer).wait_recv())
    kmix[...] = ks_q[...]

    def stale_quarter_step(t, carry):
        i = first_q + t
        kmix[i] = kv_q[i]
        att_q[t] = stale_tile(qd_q[t], kmix[...].reshape(TOKENS, 128))
        kmix[i] = ks_q[i]
        return carry

    lax.fori_loop(0, 2, stale_quarter_step, 0)
    send_rows(1, att_q, home_t)

    core_copy.wait()

    def core_add(q, carry):
        grads[core, q] = (grads[core, q].astype(F32) + from_core[q].astype(F32)).astype(BF)
        return carry

    lax.fori_loop(0, N_PATCH, core_add, 0)

    def y_copy(off):
        peer = lax.rem(yy + off, 4)
        return pltpu.make_async_remote_copy(
            src_ref=grads.at[core, :, pl.ds(pl.multiple_of(SLOT * peer, 16), SLOT)],
            dst_ref=from_y.at[off - 1],
            send_sem=ysend.at[off - 1], recv_sem=yrecv.at[off - 1],
            device_id=(4 * peer + 2 * zlo + core, me), device_id_type=MESH,
        )

    for off in range(1, 4):
        y_copy(off).start()

    dquery = gather_heads(home_a, 0)
    dkey = gather_heads(home_d, 0)
    gradx_ref[0] = (
        dot(dquery, wq[...], NT) + dot(dkey, wk[...], NT) + dot(dvalue, wv[...], NT)
    ).astype(BF)
    peers(lambda peer: come_home(3, home_t, peer).wait_recv())
    receive_rows(1, home_t)
    for r in range(2):
        rows = slice(r * ROWS // 2, (r + 1) * ROWS // 2)
        mixed_ref[0, rows] = dot(gather_heads(home_t, r * HEAD_DIM), wo[...]).astype(BF)

    for off in range(1, 4):
        y_copy(off).wait_recv()

    def y_add(q, carry):
        total = grads[core, q, pl.ds(pl.multiple_of(SLOT * yy, 16), SLOT)].astype(F32)
        for n in range(3):
            total = total + from_y[n, q].astype(F32)
        ysum[q, :SLOT] = total.astype(BF)
        ysum[q, SLOT:] = jnp.zeros((2 * HALF - SLOT, 128), BF)
        return carry

    lax.fori_loop(0, N_PATCH, y_add, 0)

    plane = zlo * N_PATCH + me

    def xz_peer(off):
        there = lax.rem(plane + off, 16)
        z_there, p_there = there // N_PATCH, lax.rem(there, N_PATCH)
        return there, z_there, p_there

    def xz_send(off):
        there, z_there, p_there = xz_peer(off)
        return pltpu.make_async_remote_copy(
            src_ref=ysum.at[p_there, pl.ds(pl.multiple_of(HALF * z_there, 16), HALF)],
            dst_ref=from_xz.at[plane],
            send_sem=xsend.at[there], recv_sem=xrecv.at[plane],
            device_id=(4 * yy + 2 * z_there + core, p_there), device_id_type=MESH,
        )

    def xz_recv(off):
        there, z_there, p_there = xz_peer(off)
        return pltpu.make_async_remote_copy(
            src_ref=from_xz.at[there], dst_ref=from_xz.at[there],
            send_sem=xsend.at[there], recv_sem=xrecv.at[there],
            device_id=(4 * yy + 2 * z_there + core, p_there), device_id_type=MESH,
        )

    def loop(lo, hi, fn):
        def step(n, carry):
            fn(n)
            return carry

        lax.fori_loop(lo, hi, step, 0)

    loop(1, 16, lambda off: xz_send(off).start())
    from_xz[plane] = ysum[me, pl.ds(pl.multiple_of(HALF * zlo, 16), HALF)]
    loop(1, 16, lambda off: xz_recv(off).wait_recv())
    total = from_xz[0].astype(F32)
    for n in range(1, 16):
        total = total + from_xz[n].astype(F32)
    gathered[img] = total.astype(BF)

    def gather_send(off):
        peer = lax.rem(img + off, N_IMG)
        return pltpu.make_async_remote_copy(
            src_ref=gathered.at[img], dst_ref=gathered.at[img],
            send_sem=gsend.at[peer], recv_sem=grecv.at[img],
            device_id=(peer, me), device_id_type=MESH,
        )

    def gather_recv(off):
        peer = lax.rem(img + off, N_IMG)
        return pltpu.make_async_remote_copy(
            src_ref=gathered.at[peer], dst_ref=gathered.at[peer],
            send_sem=gsend.at[peer], recv_sem=grecv.at[peer],
            device_id=(peer, me), device_id_type=MESH,
        )

    loop(1, N_IMG, lambda off: gather_send(off).start())
    loop(1, N_IMG, lambda off: gather_recv(off).wait_recv())
    for kind in range(2):
        for n in range(4):
            final[kind, SLOT * n : SLOT * n + HALF] = gathered[4 * n + kind].astype(F32)
            final[kind, SLOT * n + HALF : SLOT * (n + 1)] = gathered[4 * n + 2 + kind][
                : SLOT - HALF
            ].astype(F32)
    for c in range(5):
        gv_ref[:, 128 * c : 128 * c + 128] = final[0, 160 * c : 160 * c + 160]
    for c in range(10):
        go_ref[:, 128 * c : 128 * c + 128] = final[1, 80 * c : 80 * c + 80]

    for kind, (stage, land) in enumerate(((st_kv, kv_w), (st_qd, qd_w), (st_ks, ks_w))):
        peers(lambda peer: to_whole(kind, stage, land, peer).wait_send())
    for kind, stage, land in ((0, st_kv, kv_q), (2, st_ks, ks_q)):
        peers(lambda peer: to_quarter(kind, stage, land, peer).wait_send())
    for e in range(2):
        peer, copy = quarter_rows(e)

        @pl.when(peer != me)
        def _():
            copy.wait_send()

    for kind, src, land in ((0, out_w, home_a), (1, dkv_w, home_d), (2, dkv_q, home_p), (3, att_w, home_t)):
        peers(lambda peer: go_home(kind, src, land, peer).wait_send())
    for kind, src, land in ((0, out_q, home_a), (1, att_q, home_t)):
        for t in range(2):
            peer, copy = go_home_rows(kind, src, land, t)

            @pl.when(peer != me)
            def _():
                copy.wait_send()

    for off in range(1, 4):
        y_copy(off).wait_send()
    loop(1, 16, lambda off: xz_send(off).wait_send())
    loop(1, N_IMG, lambda off: gather_send(off).wait_send())


def vm(*shape, dtype=BF):
    return pltpu.VMEM(shape, dtype)


def dma(*shape):
    return pltpu.SemaphoreType.DMA(shape)


def on_device(latents_now, latents_stale, w_query, w_key, w_value, w_out, cotangent):
    return pl.pallas_call(
        kernel,
        out_shape=(
            jax.ShapeDtypeStruct((1, ROWS, C), BF),
            jax.ShapeDtypeStruct((1, ROWS, C), BF),
            jax.ShapeDtypeStruct((C // N_PATCH, INNER), F32),
            jax.ShapeDtypeStruct((INNER // N_PATCH, C), F32),
        ),
        in_specs=[pl.BlockSpec(memory_space=pl.ANY)] * 7,
        out_specs=[pl.BlockSpec(memory_space=pltpu.VMEM)] * 4,
        scratch_shapes=[
            vm(ROWS, C), vm(ROWS, C), vm(C, INNER), vm(C, INNER), vm(C, INNER), vm(INNER, C), vm(ROWS, C),
            dma(7),
            vm(10, ROWS, 128), vm(10, ROWS, 128), vm(10, ROWS, 128),
            vm(8, ROWS, 128), vm(8, ROWS, 128), vm(8, ROWS, 128),
            vm(8, ROWS, 128), vm(2, ROWS, 128), vm(8, ROWS, 128),
            dma(3, 8), dma(3, 8), dma(3, 8), dma(3, 8), dma(1),
            vm(HEAD_DIM, TOKENS, dtype=F32), vm(HEAD_DIM, TOKENS, dtype=F32),
            vm(8, ROWS, 128), vm(8, ROWS, 128), vm(2, ROWS, 128),
            vm(8, ROWS, 128), vm(8, ROWS, 128), vm(8, ROWS // 2, 128), vm(2, ROWS // 2, 128),
            vm(10, ROWS, 128), vm(10, ROWS, 128), vm(8, ROWS, 128), vm(10, ROWS // 2, 128),
            dma(4, 8), dma(4, 8), dma(2, 2), dma(2, 2),
            vm(2, 8, PART, 128), vm(8, PART, 128), vm(3, 8, SLOT, 128), vm(8, 2 * HALF, 128),
            vm(16, HALF, 128), vm(16, HALF, 128), vm(2, PART, 128, dtype=F32),
            dma(2), dma(3), dma(3), dma(16), dma(16), dma(16), dma(16),
        ],
        compiler_params=pltpu.CompilerParams(
            collective_id=0, has_side_effects=True, vmem_limit_bytes=56 * 2**20
        ),
        cost_estimate=pl.CostEstimate(flops=10**10, bytes_accessed=12 * 2**20, transcendentals=10**7),
    )(latents_now[0], latents_stale[0], w_query, w_key, w_value, w_out, cotangent[0])


def solution(mesh):
    rows = P("img", "patch", None)
    return jax.shard_map(
        on_device,
        mesh=mesh,
        in_specs=(rows, rows, P(), P(), P(), P(), rows),
        out_specs=(rows, rows, P("patch", None), P("patch", None)),
        check_vma=False,
    )
```

time: 695 us -> 116 us (0.17)
  waiting for transfers between devices: 535 us -> 0 us
  Pallas kernels: 0 us -> 111 us
  matrix products: 102 us -> 0 us
  local copies, waits for them, and re-layouts: 31.4 us -> 4.43 us
  between operations: 14 us -> 0.67 us
  other arithmetic: 10.6 us -> 0 us
    reduce_scatter x3 -> x0, waiting for transfers between devices: 231 us -> none  [the longest x1 80 us: on_device(): lax.psum_scatter(dkey_part, 'patch', scatter_dimension=0, tiled=True)]
    all_gather x4 -> x0, waiting for transfers between devices: 192 us -> none  [the longest x1 61.5 us: on_device(): lax.all_gather(key_old, 'patch', axis=0, tiled=True)]
    psum x1 -> x0, waiting for transfers between devices: 112 us -> none  [on_device(): lax.psum(grad_v.astype(jnp.bfloat16), 'img').astype(jnp.float32)]
    pallas_call x0 -> x1, Pallas kernels: none -> 111 us  [on_device(): pl.pallas_call(kernel, out_shape=(jax.ShapeDtypeStruct((1, ROWS, C), BF),...]
    dot_general x18 -> x0, matrix products: 78.9 us -> none  [the longest x5 13.3 us: project(): jnp.dot(a, w, preferred_element_type=jnp.float32).astype(jnp.bfloat16)]
    sub x2 -> x0, matrix products: 23.1 us -> none  [the longest x1 11.6 us: on_device(): prob = jax.nn.softmax(fresh, axis=-1)]
    convert_element_type x2 -> x0, other arithmetic: 10.6 us -> none  [the longest x1 8.87 us: on_device(): prob16 = prob.astype(jnp.bfloat16)]
    all_gather x2 -> x0, local copies, waits for them, and re-layouts: 9.04 us -> none  [the longest x1 4.55 us: on_device(): lax.all_gather(key_new, 'patch', axis=0, tiled=True)]
  transfers between devices with their start and end apart: 9 -> 0, of which waited for: 8 -> 0; matrix products, arithmetic and copies ran while one was open for 19% -> 0% of each run, Pallas kernels for 0% -> 0%
where the time goes in v1:
time: 116 us
  Pallas kernels  111 us (96%)
  local copies, waits for them, and re-layouts  4.43 us (4%)
    pallas_call x1, Pallas kernels, on_device(): pl.pallas_call(kernel, out_shape=(jax.ShapeDtypeStruct((1, ROWS, C), BF),...  111 us
    unnamed x10, local copies, waits for them, and re-layouts  4.43 us

profile of v1, /device:TPU:1, one launch (start us, length us, event | category | flops | bytes accessed | tf_op | source)
XLA Modules:
  0.0 115.7 jit_solution(7208222173775828197)
XLA Ops:
  0.6 110.6 %shard_map.102 = (bf16[1,256,1280]{2,1,0:T(8,128)(2,1)}, bf16[1,256,1280]{2,1,0:T(8,128)(2,1)}, f32[160,640]{1,0:T(8,128)}, f32[80,1280]{1,0:T(8,128)}) custom-call(bf16[256,1280]{1,0:T(8,128)(2,1)} %bitcast.3, bf16[256,1280]{1,0:T(8,128)(2,1)} %bitcast.4, bf16[1280,640]{1,0:T(8,128)(2,1)} %wq_hbm.1, bf16[1280,640]{1,0:T(8,128)(2,1)} %wk_hbm.1, ...), custom_call_target="tpu_custom_call" | custom-call | flops 10000000000 | bytes 12582912 | tf_op jit(solution)/shard_map/pallas_call | solution.py:517
  111.2 0.0 copy-start
  111.2 0.0 copy-start.2
  111.2 0.0 copy-start.1
  111.2 2.1 %copy.15 = bf16[1,256,1280]{2,1,0:T(8,128)(2,1)} copy(bf16[1,256,1280]{2,1,0:T(8,128)(2,1)} %get-tuple-element.8) | data formatting | bytes 1310720
  113.3 0.0 copy-done
  113.3 0.8 copy.16
  114.2 0.0 copy-done.2
  114.2 0.8 copy.17
  114.9 0.0 copy-done.1
  114.9 0.8 copy.18
Async XLA Ops:
  111.2 2.1 %copy-start = (bf16[1,256,1280]{2,1,0:T(8,128)(2,1)S(1)}, bf16[1,256,1280]{2,1,0:T(8,128)(2,1)}, u32[]{:S(2)}) copy-start(bf16[1,256,1280]{2,1,0:T(8,128)(2,1)} %get-tuple-element.9) | copy-start | bytes 1966084
  111.2 2.9 %copy-start.2 = (f32[160,640]{1,0:T(8,128)S(1)}, f32[160,640]{1,0:T(8,128)}, u32[]{:S(2)}) copy-start(f32[160,640]{1,0:T(8,128)} %get-tuple-element.10) | copy-start | bytes 1228804
  111.2 3.7 %copy-start.1 = (f32[80,1280]{1,0:T(8,128)S(1)}, f32[80,1280]{1,0:T(8,128)}, u32[]{:S(2)}) copy-start(f32[80,1280]{1,0:T(8,128)} %get-tuple-element.11) | copy-start | bytes 1228804

commit v2 on v1

v2 whole, which is shorter than its diff:
```python
import jax
import jax.numpy as jnp
from jax import lax
from jax.experimental import pallas as pl
from jax.experimental.pallas import tpu as pltpu
from jax.sharding import PartitionSpec as P

HEADS = 10
HEAD_DIM = 64
N_PATCH = 8
N_IMG = 16
ROWS = 256
TOKENS = 2048
C = 1280
INNER = 640
PART = 832
SLOT = 208
HALF = 112
BF = jnp.bfloat16
F32 = jnp.float32
MESH = pl.DeviceIdType.MESH
NT = (((1,), (1,)), ((), ()))
NN = (((1,), (0,)), ((), ()))
SCALE = HEAD_DIM**-0.5
EXP2_SCALE = SCALE * 1.4426950408889634


def dot(a, b, dims=NN):
    return lax.dot_general(a, b, dims, preferred_element_type=F32)


def left_half(rows):
    return lax.broadcasted_iota(jnp.int32, (rows, 128), 1) < HEAD_DIM


def pair(a, b):
    return jnp.concatenate([a, b], axis=1)


def fold(x, lo):
    cols = slice(lo, lo + HEAD_DIM)
    return pair(x[: ROWS // 2, cols], x[ROWS // 2 :, cols])


def probabilities(qd, kv):
    left = left_half(ROWS)
    scores = dot(jnp.where(left, qd, jnp.zeros_like(qd)), kv, NT)
    top = jnp.max(scores, axis=1, keepdims=True)
    e = jnp.exp2((scores - top) * EXP2_SCALE)
    inv = 1.0 / jnp.sum(e, axis=1, keepdims=True)
    return e.astype(BF), inv


def fresh_first(qd, kv, acc):
    left = left_half(ROWS)
    e16, inv = probabilities(qd, kv)
    a16 = (dot(e16, kv) * inv).astype(BF)
    delta = jnp.sum(
        jnp.where(left, 0.0, a16.astype(F32) * qd.astype(F32)), axis=1, keepdims=True
    )
    scaled = (qd.astype(F32) * jnp.where(left, inv * SCALE, inv)).T.astype(BF)
    acc[...] += dot(scaled[HEAD_DIM:], e16)
    return e16, fold(a16, HEAD_DIM), jnp.where(left, inv * SCALE, delta), scaled[:HEAD_DIM]


def fresh_second(qd, kv, e16, stats, q_scaled, acc):
    left = left_half(ROWS)
    dprob = dot(jnp.where(left, jnp.zeros_like(qd), qd), kv, NT)
    ds = (e16.astype(F32) * (dprob - stats[:, HEAD_DIM : HEAD_DIM + 1])).astype(BF)
    dq = dot(ds, kv) * stats[:, 0:1]
    acc[...] += dot(q_scaled, ds)
    return fold(dq.astype(BF), 0)


def stale_tile(qd, kv):
    e16, inv = probabilities(qd, kv)
    return fold((dot(e16, kv) * inv).astype(BF), HEAD_DIM)


def loop(lo, hi, fn):
    def step(n, carry):
        fn(n)
        return carry

    lax.fori_loop(lo, hi, step, 0)


def kernel(
    x_hbm, s_hbm, wq_hbm, wk_hbm, wv_hbm, wo_hbm, g_hbm,
    mixed_out, gradx_out, gv_out, go_out,
    x2, g2, s, wq, wk, wv, wo, load_sem, share_sem,
    st_kv, st_qd, st_ks,
    kv_w, qd_w, ks_w, kv_q, qd_q, ks_q,
    send_w, recv_w, send_q, recv_q,
    e_w, e_q, stats, q_scaled, acc, kmix,
    out_a, out_dq, out_t, out_dv, out_dk, part_dv, part_dk, row_a, row_dq, row_t,
    home_a, home_dq, home_t, home_dv, home_dk, home_dvp, home_dkp,
    hsend, hrecv, psend, precv, asend, arecv, apsend, aprecv,
    x_t, dv2, grads, from_y, ysum, from_xz, gathered, final,
    mixed, gradx, gv, go,
    dsem, ysend, yrecv, xsend, xrecv, gsend, grecv, out_sem,
):
    img = lax.axis_index("img")
    me = lax.axis_index("patch")
    core = lax.rem(img, 2)
    zlo = lax.rem(img // 2, 2)
    yy = img // 4
    mine_e = me // 4
    first_q = 2 * lax.rem(me, 4)
    core_one = img - core + 1
    sibling = img + 1 - 2 * core

    loads = []
    for n, (src, dst) in enumerate(
        ((x_hbm, x2.at[core]), (wk_hbm, wk), (wv_hbm, wv), (wq_hbm, wq), (g_hbm, g2.at[core]), (wo_hbm, wo), (s_hbm, s))
    ):
        copy = pltpu.make_async_copy(src, dst, load_sem.at[n])
        copy.start()
        loads.append(copy)

    barrier = pltpu.get_barrier_semaphore()
    for off in range(1, N_PATCH):
        pl.semaphore_signal(
            barrier, inc=1, device_id=(img, lax.rem(me + off, N_PATCH)), device_id_type=MESH
        )
    for off in range(1, N_IMG):
        pl.semaphore_signal(
            barrier, inc=1, device_id=(lax.rem(img + off, N_IMG), me), device_id_type=MESH
        )
    for off in range(1, N_PATCH):
        for there in (img + 2 - 4 * zlo, sibling):
            pl.semaphore_signal(
                barrier, inc=1, device_id=(there, lax.rem(me + off, N_PATCH)), device_id_type=MESH
            )

    def peers(fn):
        for dz, dx in ((1, 1), (0, 1), (1, 3), (0, 3), (1, 0), (1, 2), (0, 2)):
            fn(lax.rem(me // 4 + dz, 2) * 4 + lax.rem(me + dx, 4))

    def to_whole(kind, stage, land, peer):
        return pltpu.make_async_remote_copy(
            src_ref=stage.at[peer], dst_ref=land.at[me],
            send_sem=send_w.at[kind, peer], recv_sem=recv_w.at[kind, me],
            device_id=(img, peer), device_id_type=MESH,
        )

    def from_whole(kind, land, peer):
        return pltpu.make_async_remote_copy(
            src_ref=land.at[peer], dst_ref=land.at[peer],
            send_sem=send_w.at[kind, peer], recv_sem=recv_w.at[kind, peer],
            device_id=(img, peer), device_id_type=MESH,
        )

    def to_quarter(kind, stage, land, peer):
        return pltpu.make_async_remote_copy(
            src_ref=stage.at[N_PATCH + peer // 4], dst_ref=land.at[me],
            send_sem=send_q.at[kind, peer], recv_sem=recv_q.at[kind, me],
            device_id=(img, peer), device_id_type=MESH,
        )

    def from_quarter(kind, land, peer):
        return pltpu.make_async_remote_copy(
            src_ref=land.at[peer], dst_ref=land.at[peer],
            send_sem=send_q.at[kind, peer], recv_sem=recv_q.at[kind, peer],
            device_id=(img, peer), device_id_type=MESH,
        )

    def quarter_rows(e):
        peer = 4 * e + me // 2
        return peer, pltpu.make_async_remote_copy(
            src_ref=st_qd.at[N_PATCH + e], dst_ref=qd_q.at[lax.rem(me, 2)],
            send_sem=send_q.at[1, e], recv_sem=recv_q.at[1, lax.rem(me, 2)],
            device_id=(img, peer), device_id_type=MESH,
        )

    def quarter_rows_in(t):
        return first_q + t, pltpu.make_async_remote_copy(
            src_ref=qd_q.at[t], dst_ref=qd_q.at[t],
            send_sem=send_q.at[1, t], recv_sem=recv_q.at[1, t],
            device_id=(img, first_q + t), device_id_type=MESH,
        )

    def share(core_from, ref, n):
        return pltpu.make_async_remote_copy(
            src_ref=ref.at[core_from], dst_ref=ref.at[core_from],
            send_sem=share_sem.at[n], recv_sem=share_sem.at[2 + n],
            device_id=(sibling, me), device_id_type=MESH,
        )

    def stage_pairs(stage, a, b):
        for h in range(HEADS):
            cols = slice(h * HEAD_DIM, (h + 1) * HEAD_DIM)
            stage[h] = pair(a[:, cols], b[:, cols])

    loads[0].wait()
    loads[1].wait()
    key = dot(x2[core], wk[...]).astype(BF)
    loads[2].wait()
    value = dot(x2[core], wv[...]).astype(BF)
    stage_pairs(st_kv, key, value)
    pl.semaphore_wait(barrier, 3 * (N_PATCH - 1) + N_IMG - 1)
    peers(lambda peer: to_whole(0, st_kv, kv_w, peer).start())
    kv_w[me] = st_kv[me]
    loads[3].wait()
    query = dot(x2[core], wq[...]).astype(BF)
    loads[4].wait()
    loads[5].wait()
    dattend = dot(g2[core], wo[...], NT).astype(BF)
    stage_pairs(st_qd, query, dattend)
    peers(lambda peer: to_whole(1, st_qd, qd_w, peer).start())
    qd_w[me] = st_qd[me]
    peers(lambda peer: to_quarter(0, st_kv, kv_q, peer).start())
    kv_q[me] = st_kv[N_PATCH + mine_e]
    for e in range(2):
        peer, copy = quarter_rows(e)

        @pl.when(peer != me)
        def _():
            copy.start()

        @pl.when(peer == me)
        def _():
            qd_q[lax.rem(me, 2)] = st_qd[N_PATCH + e]

    @pl.when(core == 1)
    def _():
        share(1, x2, 0).start()

    @pl.when(core == 0)
    def _():
        share(0, g2, 1).start()

    loads[6].wait()
    key_old = dot(s[...], wk[...]).astype(BF)
    value_old = dot(s[...], wv[...]).astype(BF)
    stage_pairs(st_ks, key_old, value_old)
    ks_w[me] = st_ks[me]
    ks_q[me] = st_ks[N_PATCH + mine_e]

    @pl.when(core == 0)
    def _():
        share(1, x2, 0).wait_recv()
        x_t[:, :ROWS] = x2[0].T
        x_t[:, ROWS:] = x2[1].T

    @pl.when(core == 1)
    def _():
        share(0, g2, 1).wait_recv()

    def go_home(kind, src, land, peer):
        return pltpu.make_async_remote_copy(
            src_ref=src.at[peer], dst_ref=land.at[me],
            send_sem=hsend.at[kind, peer], recv_sem=hrecv.at[kind, me],
            device_id=(img, peer), device_id_type=MESH,
        )

    def come_home(kind, land, peer):
        return pltpu.make_async_remote_copy(
            src_ref=land.at[peer], dst_ref=land.at[peer],
            send_sem=hsend.at[kind, peer], recv_sem=hrecv.at[kind, peer],
            device_id=(img, peer), device_id_type=MESH,
        )

    def go_home_rows(kind, src, land, t):
        peer = first_q + t
        return peer, pltpu.make_async_remote_copy(
            src_ref=src.at[t], dst_ref=land.at[N_PATCH + mine_e],
            send_sem=psend.at[kind, t], recv_sem=precv.at[kind, mine_e],
            device_id=(img, peer), device_id_type=MESH,
        )

    def come_home_rows(kind, land, e):
        peer = 4 * e + me // 2
        return peer, pltpu.make_async_remote_copy(
            src_ref=land.at[N_PATCH + e], dst_ref=land.at[N_PATCH + e],
            send_sem=psend.at[kind, e], recv_sem=precv.at[kind, e],
            device_id=(img, peer), device_id_type=MESH,
        )

    def a_home(i):
        return pltpu.make_async_remote_copy(
            src_ref=out_a.at[i], dst_ref=home_a.at[core, me],
            send_sem=asend.at[i], recv_sem=arecv.at[core, me],
            device_id=(core_one, i), device_id_type=MESH,
        )

    def a_in(c, peer):
        return pltpu.make_async_remote_copy(
            src_ref=home_a.at[c, peer], dst_ref=home_a.at[c, peer],
            send_sem=asend.at[peer], recv_sem=arecv.at[c, peer],
            device_id=(core_one, peer), device_id_type=MESH,
        )

    def a_home_rows(t):
        return pltpu.make_async_remote_copy(
            src_ref=row_a.at[t], dst_ref=home_a.at[core, N_PATCH + mine_e],
            send_sem=apsend.at[t], recv_sem=aprecv.at[core, mine_e],
            device_id=(core_one, first_q + t), device_id_type=MESH,
        )

    def a_in_rows(c, e):
        return pltpu.make_async_remote_copy(
            src_ref=home_a.at[c, N_PATCH + e], dst_ref=home_a.at[c, N_PATCH + e],
            send_sem=apsend.at[e], recv_sem=aprecv.at[c, e],
            device_id=(core_one, 4 * e + me // 2), device_id_type=MESH,
        )

    def stays(peer):
        return jnp.logical_and(peer == me, core == 1)

    def put(out):
        for j in range(N_PATCH):
            out[j] = fold(acc[:, j * ROWS : (j + 1) * ROWS].T.astype(BF), 0)

    def clear():
        acc[...] = jnp.zeros_like(acc)

    peers(lambda peer: from_whole(0, kv_w, peer).wait_recv())
    peers(lambda peer: from_whole(1, qd_w, peer).wait_recv())
    clear()

    def first_whole(i):
        e_w[i], out_a[i], stats[i], q_scaled[i] = fresh_first(
            qd_w[i], kv_w[...].reshape(TOKENS, 128), acc
        )

        @pl.when(jnp.logical_not(stays(i)))
        def _():
            a_home(i).start()

    loop(0, N_PATCH, first_whole)

    @pl.when(core == 1)
    def _():
        home_a[1, me] = out_a[me]

    put(out_dv)
    peers(lambda peer: go_home(3, out_dv, home_dv, peer).start())
    home_dv[me] = out_dv[me]
    peers(lambda peer: to_whole(2, st_ks, ks_w, peer).start())

    peers(lambda peer: from_quarter(0, kv_q, peer).wait_recv())
    for t in range(2):
        peer, copy = quarter_rows_in(t)

        @pl.when(peer != me)
        def _():
            copy.wait_recv()

    clear()

    def first_quarter(t):
        e_q[t], row_a[t], stats[N_PATCH + t], q_scaled[N_PATCH + t] = fresh_first(
            qd_q[t], kv_q[...].reshape(TOKENS, 128), acc
        )

    loop(0, 2, first_quarter)
    for t in range(2):
        here = stays(first_q + t)

        @pl.when(jnp.logical_not(here))
        def _():
            a_home_rows(t).start()

        @pl.when(here)
        def _():
            home_a[1, N_PATCH + mine_e] = row_a[t]

    put(part_dv)
    peers(lambda peer: go_home(5, part_dv, home_dvp, peer).start())
    home_dvp[me] = part_dv[me]
    peers(lambda peer: to_quarter(2, st_ks, ks_q, peer).start())

    clear()

    def second_whole(i):
        out_dq[i] = fresh_second(
            qd_w[i], kv_w[...].reshape(TOKENS, 128), e_w[i], stats[i], q_scaled[i], acc
        )

        @pl.when(i != me)
        def _():
            go_home(0, out_dq, home_dq, i).start()

    loop(0, N_PATCH, second_whole)
    home_dq[me] = out_dq[me]
    put(out_dk)
    peers(lambda peer: go_home(1, out_dk, home_dk, peer).start())
    home_dk[me] = out_dk[me]

    def unfold(src, r):
        cols = slice(r * HEAD_DIM, (r + 1) * HEAD_DIM)
        return jnp.concatenate([src[h][:, cols] for h in range(HEADS)], axis=1)

    def add_shared(land, parts):
        for e in range(2):
            total = parts[4 * e].astype(F32)
            for n in range(1, 4):
                total = total + parts[4 * e + n].astype(F32)
            land[N_PATCH + e] = total.astype(BF)

    peers(lambda peer: come_home(3, home_dv, peer).wait_recv())
    peers(lambda peer: come_home(5, home_dvp, peer).wait_recv())
    add_shared(home_dv, home_dvp)
    for r in range(2):
        dv2[core, r * ROWS // 2 : (r + 1) * ROWS // 2] = unfold(home_dv, r)
    dv_share = pltpu.make_async_remote_copy(
        src_ref=dv2.at[1], dst_ref=dv2.at[1], send_sem=dsem.at[0], recv_sem=dsem.at[1],
        device_id=(sibling, me), device_id_type=MESH,
    )

    @pl.when(core == 1)
    def _():
        dv_share.start()
        for c in range(2):
            for n in range(N_PATCH):
                if c == 1:
                    @pl.when(n != me)
                    def _():
                        a_in(c, n).wait_recv()
                else:
                    a_in(c, n).wait_recv()
            for e in range(2):
                if c == 1:
                    @pl.when(4 * e + me // 2 != me)
                    def _():
                        a_in_rows(c, e).wait_recv()
                else:
                    a_in_rows(c, e).wait_recv()
        a_t = jnp.concatenate(
            [unfold(home_a.at[c], r).T for c in range(2) for r in range(2)], axis=1
        )
        g_all = g2[...].reshape(2 * ROWS, C)
        for q in range(N_PATCH):
            part = dot(a_t[80 * q : 80 * q + 80], g_all).astype(BF)
            for c in range(10):
                grads[q, 80 * c : 80 * c + 80] = part[:, 128 * c : 128 * c + 128]

    @pl.when(core == 0)
    def _():
        dv_share.wait_recv()
        dv_all = dv2[...].reshape(2 * ROWS, INNER)
        for q in range(N_PATCH):
            part = dot(x_t[160 * q : 160 * q + 160], dv_all).astype(BF)
            for c in range(5):
                grads[q, 160 * c : 160 * c + 160] = part[:, 128 * c : 128 * c + 128]

    grads[:, 800:] = jnp.zeros((N_PATCH, PART - 800, 128), BF)

    def y_copy(off):
        peer = lax.rem(yy + off, 4)
        return pltpu.make_async_remote_copy(
            src_ref=grads.at[:, pl.ds(pl.multiple_of(SLOT * peer, 16), SLOT)],
            dst_ref=from_y.at[off - 1],
            send_sem=ysend.at[off - 1], recv_sem=yrecv.at[off - 1],
            device_id=(4 * peer + 2 * zlo + core, me), device_id_type=MESH,
        )

    for off in range(1, 4):
        y_copy(off).start()

    clear()

    def second_quarter(t):
        row_dq[t] = fresh_second(
            qd_q[t], kv_q[...].reshape(TOKENS, 128), e_q[t], stats[N_PATCH + t],
            q_scaled[N_PATCH + t], acc,
        )

    loop(0, 2, second_quarter)

    def send_rows(kind, src, land):
        for t in range(2):
            peer, copy = go_home_rows(kind, src, land, t)

            @pl.when(peer != me)
            def _():
                copy.start()

            @pl.when(peer == me)
            def _():
                land[N_PATCH + mine_e] = src[t]

    send_rows(0, row_dq, home_dq)
    put(part_dk)
    peers(lambda peer: go_home(4, part_dk, home_dkp, peer).start())
    home_dkp[me] = part_dk[me]

    peers(lambda peer: from_whole(2, ks_w, peer).wait_recv())
    kmix[...] = ks_w[...]

    def stale_whole(i):
        kmix[i] = kv_w[i]
        out_t[i] = stale_tile(qd_w[i], kmix[...].reshape(TOKENS, 128))
        kmix[i] = ks_w[i]

        @pl.when(i != me)
        def _():
            go_home(2, out_t, home_t, i).start()

    loop(0, N_PATCH, stale_whole)
    home_t[me] = out_t[me]
    peers(lambda peer: from_quarter(2, ks_q, peer).wait_recv())
    kmix[...] = ks_q[...]

    def stale_quarter(t):
        i = first_q + t
        kmix[i] = kv_q[i]
        row_t[t] = stale_tile(qd_q[t], kmix[...].reshape(TOKENS, 128))
        kmix[i] = ks_q[i]

    loop(0, 2, stale_quarter)
    send_rows(1, row_t, home_t)

    for off in range(1, 4):
        y_copy(off).wait_recv()

    def y_add(q):
        total = grads[q, pl.ds(pl.multiple_of(SLOT * yy, 16), SLOT)].astype(F32)
        for n in range(3):
            total = total + from_y[n, q].astype(F32)
        ysum[q, :SLOT] = total.astype(BF)
        ysum[q, SLOT:] = jnp.zeros((2 * HALF - SLOT, 128), BF)

    loop(0, N_PATCH, y_add)
    plane = zlo * N_PATCH + me

    def xz_peer(off):
        there = lax.rem(plane + off, 16)
        return there, there // N_PATCH, lax.rem(there, N_PATCH)

    def xz_send(off):
        there, z_there, p_there = xz_peer(off)
        return pltpu.make_async_remote_copy(
            src_ref=ysum.at[p_there, pl.ds(pl.multiple_of(HALF * z_there, 16), HALF)],
            dst_ref=from_xz.at[plane],
            send_sem=xsend.at[there], recv_sem=xrecv.at[plane],
            device_id=(4 * yy + 2 * z_there + core, p_there), device_id_type=MESH,
        )

    def xz_recv(off):
        there, z_there, p_there = xz_peer(off)
        return pltpu.make_async_remote_copy(
            src_ref=from_xz.at[there], dst_ref=from_xz.at[there],
            send_sem=xsend.at[there], recv_sem=xrecv.at[there],
            device_id=(4 * yy + 2 * z_there + core, p_there), device_id_type=MESH,
        )

    loop(1, 16, lambda off: xz_send(off).start())
    from_xz[plane] = ysum[me, pl.ds(pl.multiple_of(HALF * zlo, 16), HALF)]

    def receive_rows(kind, land):
        for e in range(2):
            peer, copy = come_home_rows(kind, land, e)

            @pl.when(peer != me)
            def _():
                copy.wait_recv()

    peers(lambda peer: come_home(0, home_dq, peer).wait_recv())
    receive_rows(0, home_dq)
    peers(lambda peer: come_home(1, home_dk, peer).wait_recv())
    peers(lambda peer: come_home(4, home_dkp, peer).wait_recv())
    add_shared(home_dk, home_dkp)
    dquery = jnp.concatenate([unfold(home_dq, 0), unfold(home_dq, 1)], axis=0)
    dkey = jnp.concatenate([unfold(home_dk, 0), unfold(home_dk, 1)], axis=0)
    gradx[...] = (
        dot(dquery, wq[...], NT) + dot(dkey, wk[...], NT) + dot(dv2[core], wv[...], NT)
    ).astype(BF)
    gradx_copy = pltpu.make_async_copy(gradx, gradx_out.at[0], out_sem.at[0])
    gradx_copy.start()

    loop(1, 16, lambda off: xz_recv(off).wait_recv())
    total = from_xz[0].astype(F32)
    for n in range(1, 16):
        total = total + from_xz[n].astype(F32)
    gathered[img] = total.astype(BF)

    def gather_send(off):
        peer = lax.rem(img + off, N_IMG)
        return pltpu.make_async_remote_copy(
            src_ref=gathered.at[img], dst_ref=gathered.at[img],
            send_sem=gsend.at[peer], recv_sem=grecv.at[img],
            device_id=(peer, me), device_id_type=MESH,
        )

    def gather_recv(off):
        peer = lax.rem(img + off, N_IMG)
        return pltpu.make_async_remote_copy(
            src_ref=gathered.at[peer], dst_ref=gathered.at[peer],
            send_sem=gsend.at[peer], recv_sem=grecv.at[peer],
            device_id=(peer, me), device_id_type=MESH,
        )

    loop(1, N_IMG, lambda off: gather_send(off).start())

    peers(lambda peer: come_home(2, home_t, peer).wait_recv())
    receive_rows(1, home_t)
    for r in range(2):
        mixed[r * ROWS // 2 : (r + 1) * ROWS // 2] = dot(unfold(home_t, r), wo[...]).astype(BF)
    mixed_copy = pltpu.make_async_copy(mixed, mixed_out.at[0], out_sem.at[1])
    mixed_copy.start()

    loop(1, N_IMG, lambda off: gather_recv(off).wait_recv())
    for kind in range(2):
        for n in range(4):
            final[kind, SLOT * n : SLOT * n + HALF] = gathered[4 * n + kind].astype(F32)
            final[kind, SLOT * n + HALF : SLOT * (n + 1)] = gathered[4 * n + 2 + kind][
                : SLOT - HALF
            ].astype(F32)
    for c in range(5):
        gv[:, 128 * c : 128 * c + 128] = final[0, 160 * c : 160 * c + 160]
    for c in range(10):
        go[:, 128 * c : 128 * c + 128] = final[1, 80 * c : 80 * c + 80]
    gv_copy = pltpu.make_async_copy(gv, gv_out, out_sem.at[2])
    go_copy = pltpu.make_async_copy(go, go_out, out_sem.at[3])
    gv_copy.start()
    go_copy.start()

    for kind, stage, land in ((0, st_kv, kv_w), (1, st_qd, qd_w), (2, st_ks, ks_w)):
        peers(lambda peer: to_whole(kind, stage, land, peer).wait_send())
    for kind, stage, land in ((0, st_kv, kv_q), (2, st_ks, ks_q)):
        peers(lambda peer: to_quarter(kind, stage, land, peer).wait_send())
    for e in range(2):
        peer, copy = quarter_rows(e)

        @pl.when(peer != me)
        def _():
            copy.wait_send()

    @pl.when(core == 1)
    def _():
        share(1, x2, 0).wait_send()
        dv_share.wait_send()

    @pl.when(core == 0)
    def _():
        share(0, g2, 1).wait_send()

    for kind, src, land in (
        (0, out_dq, home_dq), (1, out_dk, home_dk), (2, out_t, home_t),
        (3, out_dv, home_dv), (4, part_dk, home_dkp), (5, part_dv, home_dvp),
    ):
        peers(lambda peer: go_home(kind, src, land, peer).wait_send())
    for kind, src, land in ((0, row_dq, home_dq), (1, row_t, home_t)):
        for t in range(2):
            peer, copy = go_home_rows(kind, src, land, t)

            @pl.when(peer != me)
            def _():
                copy.wait_send()

    for n in range(N_PATCH):
        @pl.when(jnp.logical_not(stays(n)))
        def _():
            a_home(n).wait_send()

    for t in range(2):
        @pl.when(jnp.logical_not(stays(first_q + t)))
        def _():
            a_home_rows(t).wait_send()

    for off in range(1, 4):
        y_copy(off).wait_send()
    loop(1, 16, lambda off: xz_send(off).wait_send())
    loop(1, N_IMG, lambda off: gather_send(off).wait_send())
    for copy in (gradx_copy, mixed_copy, gv_copy, go_copy):
        copy.wait()


def pass_on(*refs):
    sources, results, held = refs[:4], refs[4:8], refs[8:12]
    load_sem, store_sem = refs[12:]
    loads = [pltpu.make_async_copy(sources[n], held[n], load_sem.at[n]) for n in range(4)]
    stores = [pltpu.make_async_copy(held[n], results[n], store_sem.at[n]) for n in range(4)]
    for copy in loads:
        copy.start()
    for load, store in zip(loads, stores):
        load.wait()
        store.start()
    for store in stores:
        store.wait()


def vm(*shape, dtype=BF):
    return pltpu.VMEM(shape, dtype)


def dma(*shape):
    return pltpu.SemaphoreType.DMA(shape)


def on_device(latents_now, latents_stale, w_query, w_key, w_value, w_out, cotangent):
    half = ROWS // 2
    shapes = (
        jax.ShapeDtypeStruct((1, ROWS, C), BF),
        jax.ShapeDtypeStruct((1, ROWS, C), BF),
        jax.ShapeDtypeStruct((C // N_PATCH, INNER), F32),
        jax.ShapeDtypeStruct((INNER // N_PATCH, C), F32),
    )
    anywhere = pl.BlockSpec(memory_space=pl.ANY)
    results = pl.pallas_call(
        kernel,
        out_shape=shapes,
        in_specs=[anywhere] * 7,
        out_specs=[anywhere] * 4,
        scratch_shapes=[
            vm(2, ROWS, C), vm(2, ROWS, C), vm(ROWS, C), vm(C, INNER), vm(C, INNER), vm(C, INNER), vm(INNER, C),
            dma(7), dma(4),
            vm(10, ROWS, 128), vm(10, ROWS, 128), vm(10, ROWS, 128),
            vm(8, ROWS, 128), vm(8, ROWS, 128), vm(8, ROWS, 128),
            vm(8, ROWS, 128), vm(2, ROWS, 128), vm(8, ROWS, 128),
            dma(3, 8), dma(3, 8), dma(3, 8), dma(3, 8),
            vm(8, ROWS, TOKENS), vm(2, ROWS, TOKENS), vm(10, ROWS, 128, dtype=F32), vm(10, HEAD_DIM, ROWS),
            vm(HEAD_DIM, TOKENS, dtype=F32), vm(8, ROWS, 128),
            vm(8, half, 128), vm(8, half, 128), vm(8, half, 128), vm(8, half, 128), vm(8, half, 128),
            vm(8, half, 128), vm(8, half, 128), vm(2, half, 128), vm(2, half, 128), vm(2, half, 128),
            vm(2, 10, half, 128), vm(10, half, 128), vm(10, half, 128), vm(10, half, 128), vm(10, half, 128),
            vm(8, half, 128), vm(8, half, 128),
            dma(6, 8), dma(6, 8), dma(2, 2), dma(2, 2), dma(8), dma(2, 8), dma(2), dma(2, 2),
            vm(C, 2 * ROWS), vm(2, ROWS, INNER), vm(8, PART, 128), vm(3, 8, SLOT, 128), vm(8, 2 * HALF, 128),
            vm(16, HALF, 128), vm(16, HALF, 128), vm(2, PART, 128, dtype=F32),
            vm(ROWS, C), vm(ROWS, C), vm(C // N_PATCH, INNER, dtype=F32), vm(INNER // N_PATCH, C, dtype=F32),
            dma(2), dma(3), dma(3), dma(16), dma(16), dma(16), dma(16), dma(4),
        ],
        compiler_params=pltpu.CompilerParams(
            collective_id=0, has_side_effects=True, vmem_limit_bytes=56 * 2**20
        ),
        cost_estimate=pl.CostEstimate(flops=10**10, bytes_accessed=12 * 2**20, transcendentals=10**7),
    )(latents_now[0], latents_stale[0], w_query, w_key, w_value, w_out, cotangent[0])
    return pl.pallas_call(
        pass_on,
        out_shape=shapes,
        in_specs=[anywhere] * 4,
        out_specs=[anywhere] * 4,
        scratch_shapes=[pltpu.VMEM(shape.shape, shape.dtype) for shape in shapes] + [dma(4), dma(4)],
        compiler_params=pltpu.CompilerParams(vmem_limit_bytes=16 * 2**20),
        cost_estimate=pl.CostEstimate(flops=0, bytes_accessed=2 * 2**20, transcendentals=0),
    )(*results)


def solution(mesh):
    rows = P("img", "patch", None)
    return jax.shard_map(
        on_device,
        mesh=mesh,
        in_specs=(rows, rows, P(), P(), P(), P(), rows),
        out_specs=(rows, rows, P("patch", None), P("patch", None)),
        check_vma=False,
    )
```

time: 116 us -> 104 us (0.90)
  Pallas kernels: 111 us -> 99.2 us
    pallas_call x1 -> x2, Pallas kernels: 111 us -> 99.2 us  [the longest x1 97 us: on_device(): pl.pallas_call(kernel, out_shape=shapes, in_specs=[anywhere] * 7, out_spe...]
    unnamed x10 -> x8, local copies, waits for them, and re-layouts: 4.43 us -> 4.17 us
where the time goes in v2:
time: 104 us
  Pallas kernels  99.2 us (95%)
  local copies, waits for them, and re-layouts  4.17 us (4%)
    pallas_call x1, Pallas kernels, on_device(): pl.pallas_call(kernel, out_shape=shapes, in_specs=[anywhere] * 7, out_spe...  97 us
    unnamed x8, local copies, waits for them, and re-layouts  4.17 us
    pallas_call x1, Pallas kernels, on_device(): pl.pallas_call(pass_on, out_shape=shapes, in_specs=[anywhere] * 4, out_sp...  2.21 us

profile of v2, /device:TPU:1, one launch (start us, length us, event | category | flops | bytes accessed | tf_op | source)
XLA Modules:
  0.0 104.2 jit_solution(8174080908818942211)
XLA Ops:
  0.6 97.0 %shard_map.102 = (bf16[1,256,1280]{2,1,0:T(8,128)(2,1)}, bf16[1,256,1280]{2,1,0:T(8,128)(2,1)}, f32[160,640]{1,0:T(8,128)}, f32[80,1280]{1,0:T(8,128)}) custom-call(bf16[256,1280]{1,0:T(8,128)(2,1)} %bitcast.3, bf16[256,1280]{1,0:T(8,128)(2,1)} %bitcast.4, bf16[1280,640]{1,0:T(8,128)(2,1)} %wq_hbm.1, bf16[1280,640]{1,0:T(8,128)(2,1)} %wk_hbm.1, ...), custom_call_target="tpu_custom_call" | custom-call | flops 10000000000 | bytes 12582912 | tf_op jit(solution)/shard_map/pallas_call | solution.py:702
  97.7 0.0 copy-start
  97.7 1.1 %copy-done = bf16[1,256,1280]{2,1,0:T(8,128)(2,1)S(1)} copy-done((bf16[1,256,1280]{2,1,0:T(8,128)(2,1)S(1)}, bf16[1,256,1280]{2,1,0:T(8,128)(2,1)}, u32[]{:S(2)}) %copy-start) | copy-done | bytes 655384
  98.8 0.0 copy-start.1
  98.8 1.1 %copy-done.1 = bf16[1,256,1280]{2,1,0:T(8,128)(2,1)S(1)} copy-done((bf16[1,256,1280]{2,1,0:T(8,128)(2,1)S(1)}, bf16[1,256,1280]{2,1,0:T(8,128)(2,1)}, u32[]{:S(2)}) %copy-start.1) | copy-done | bytes 655384
  99.8 0.0 copy-start.2
  99.8 1.0 copy-done.2
  100.8 0.0 copy-start.3
  100.8 1.0 copy-done.3
  101.8 2.2 %shard_map.103 = (bf16[1,256,1280]{2,1,0:T(8,128)(2,1)}, bf16[1,256,1280]{2,1,0:T(8,128)(2,1)}, f32[160,640]{1,0:T(8,128)}, f32[80,1280]{1,0:T(8,128)}) custom-call(bf16[1,256,1280]{2,1,0:T(8,128)(2,1)S(1)} %copy-done, bf16[1,256,1280]{2,1,0:T(8,128)(2,1)S(1)} %copy-done.1, f32[160,640]{1,0:T(8,128)S(1)} %copy-done.2, f32[80,1280]{1,0:T(8,128)S(1)} %copy-done.3), custom_call_target="tpu_custom_call" | custom-call | bytes 2097152 | tf_op jit(solution)/shard_map/pallas_call | solution.py:731
Async XLA Ops:
  97.7 1.1 %copy-start = (bf16[1,256,1280]{2,1,0:T(8,128)(2,1)S(1)}, bf16[1,256,1280]{2,1,0:T(8,128)(2,1)}, u32[]{:S(2)}) copy-start(bf16[1,256,1280]{2,1,0:T(8,128)(2,1)} %get-tuple-element.8.refs_0_) | copy-start | bytes 1966084
  98.8 1.1 %copy-start.1 = (bf16[1,256,1280]{2,1,0:T(8,128)(2,1)S(1)}, bf16[1,256,1280]{2,1,0:T(8,128)(2,1)}, u32[]{:S(2)}) copy-start(bf16[1,256,1280]{2,1,0:T(8,128)(2,1)} %get-tuple-element.9.refs_1_) | copy-start | bytes 1966084
  99.8 1.0 copy-start.2
  100.8 1.0 copy-start.3

commit v3 on v2

--- a/solution.py
+++ b/solution.py
@@ -94,7 +94,7 @@
     send_w, recv_w, send_q, recv_q,
     e_w, e_q, stats, q_scaled, acc, kmix,
     out_a, out_dq, out_t, out_dv, out_dk, part_dv, part_dk, row_a, row_dq, row_t,
-    home_a, home_dq, home_t, home_dv, home_dk, home_dvp, home_dkp,
+    home_a, home_dq, home_t, home_dv, home_dk, home_dvp, home_dkp, sib_dv, sib_dk, pair_send, pair_recv,
     hsend, hrecv, psend, precv, asend, arecv, apsend, aprecv,
     x_t, dv2, grads, from_y, ysum, from_xz, gathered, final,
     mixed, gradx, gv, go,
@@ -106,17 +106,28 @@
     zlo = lax.rem(img // 2, 2)
     yy = img // 4
     mine_e = me // 4
-    first_q = 2 * lax.rem(me, 4)
+    shared_core = lax.rem(me // 2, 2)
+    shared_img = img - core + shared_core
+    holds = core == shared_core
+    first_q = 4 * lax.rem(me, 2) + 2 * core
+    my_helper_core = lax.rem(me, 4) // 2
+
+    def helper(c, e):
+        return img - core + my_helper_core, 4 * e + 2 * c + me // 4
     core_one = img - core + 1
     sibling = img + 1 - 2 * core
 
-    loads = []
-    for n, (src, dst) in enumerate(
-        ((x_hbm, x2.at[core]), (wk_hbm, wk), (wv_hbm, wv), (wq_hbm, wq), (g_hbm, g2.at[core]), (wo_hbm, wo), (s_hbm, s))
-    ):
-        copy = pltpu.make_async_copy(src, dst, load_sem.at[n])
+    loads = [
+        pltpu.make_async_copy(src, dst, load_sem.at[n])
+        for n, (src, dst) in enumerate(
+            (
+                (x_hbm, x2.at[core]), (wk_hbm, wk), (wv_hbm, wv), (wq_hbm, wq),
+                (g_hbm, g2.at[core]), (wo_hbm, wo), (s_hbm, s),
+            )
+        )
+    ]
+    for copy in loads[:3]:
         copy.start()
-        loads.append(copy)
 
     barrier = pltpu.get_barrier_semaphore()
     for off in range(1, N_PATCH):
@@ -133,9 +144,13 @@
                 barrier, inc=1, device_id=(there, lax.rem(me + off, N_PATCH)), device_id_type=MESH
             )
 
+    def turn(off, sign=1):
+        dx = off % 4 if sign == 1 else 4 - off % 4
+        return lax.rem(me // 4 + off // 4, 2) * 4 + lax.rem(me + dx, 4)
+
     def peers(fn):
-        for dz, dx in ((1, 1), (0, 1), (1, 3), (0, 3), (1, 0), (1, 2), (0, 2)):
-            fn(lax.rem(me // 4 + dz, 2) * 4 + lax.rem(me + dx, 4))
+        for off in (5, 1, 7, 3, 4, 6, 2):
+            fn(turn(off))
 
     def to_whole(kind, stage, land, peer):
         return pltpu.make_async_remote_copy(
@@ -151,12 +166,32 @@
             device_id=(img, peer), device_id_type=MESH,
         )
 
-    def to_quarter(kind, stage, land, peer):
-        return pltpu.make_async_remote_copy(
-            src_ref=stage.at[N_PATCH + peer // 4], dst_ref=land.at[me],
+    def to_quarter(kind, stage, land, e, n):
+        peer = 4 * e + 2 * core + n
+        return peer, pltpu.make_async_remote_copy(
+            src_ref=stage.at[N_PATCH + e], dst_ref=land.at[me],
             send_sem=send_q.at[kind, peer], recv_sem=recv_q.at[kind, me],
             device_id=(img, peer), device_id_type=MESH,
         )
+
+    def each_quarter(fn):
+        for e in range(2):
+            for n in range(2):
+                fn(e, n)
+
+    def send_quarter(kind, stage, land):
+        def one(e, n):
+            peer, copy = to_quarter(kind, stage, land, e, n)
+
+            @pl.when(peer != me)
+            def _():
+                copy.start()
+
+        each_quarter(one)
+
+        @pl.when(holds)
+        def _():
+            land[me] = stage[N_PATCH + mine_e]
 
     def from_quarter(kind, land, peer):
         return pltpu.make_async_remote_copy(
@@ -165,19 +200,63 @@
             device_id=(img, peer), device_id_type=MESH,
         )
 
+    def hand_over(n, src, dst):
+        return pltpu.make_async_remote_copy(
+            src_ref=src, dst_ref=dst, send_sem=pair_send.at[n], recv_sem=pair_recv.at[n],
+            device_id=(sibling, me), device_id_type=MESH,
+        )
+
+    def pass_keys(n, kind, land):
+        @pl.when(holds)
+        def _():
+            peers(lambda peer: from_quarter(kind, land, peer).wait_recv())
+            hand_over(n, land, land).start()
+
+    def wait_keys(n, land):
+        @pl.when(jnp.logical_not(holds))
+        def _():
+            hand_over(n, land, land).wait_recv()
+
+    def pass_sums(n, part, arrived):
+        @pl.when(jnp.logical_not(holds))
+        def _():
+            hand_over(n, part, arrived).start()
+
+    def send_sums(n, kind, part, arrived, land):
+        @pl.when(holds)
+        def _():
+            hand_over(n, part, arrived).wait_recv()
+            part[...] = (part[...].astype(F32) + arrived[...].astype(F32)).astype(BF)
+            peers(lambda peer: go_home(kind, part, land, peer).start())
+            land[me] = part[me]
+
+    def receive_sums(kind, land):
+        def one(e, n):
+            peer = 4 * e + 2 * core + n
+
+            @pl.when(peer != me)
+            def _():
+                come_home(kind, land, peer).wait_recv()
+
+        each_quarter(one)
+
     def quarter_rows(e):
-        peer = 4 * e + me // 2
-        return peer, pltpu.make_async_remote_copy(
+        there, peer = helper(core, e)
+        here = jnp.logical_and(there == img, peer == me)
+        return here, pltpu.make_async_remote_copy(
             src_ref=st_qd.at[N_PATCH + e], dst_ref=qd_q.at[lax.rem(me, 2)],
             send_sem=send_q.at[1, e], recv_sem=recv_q.at[1, lax.rem(me, 2)],
-            device_id=(img, peer), device_id_type=MESH,
-        )
+            device_id=(there, peer), device_id_type=MESH,
+        )
+
+    def owned(t):
+        return jnp.logical_and(holds, first_q + t == me)
 
     def quarter_rows_in(t):
-        return first_q + t, pltpu.make_async_remote_copy(
+        return pltpu.make_async_remote_copy(
             src_ref=qd_q.at[t], dst_ref=qd_q.at[t],
             send_sem=send_q.at[1, t], recv_sem=recv_q.at[1, t],
-            device_id=(img, first_q + t), device_id_type=MESH,
+            device_id=(shared_img, first_q + t), device_id_type=MESH,
         )
 
     def share(core_from, ref, n):
@@ -194,6 +273,8 @@
 
     loads[0].wait()
     loads[1].wait()
+    for copy in loads[3:]:
+        copy.start()
     key = dot(x2[core], wk[...]).astype(BF)
     loads[2].wait()
     value = dot(x2[core], wv[...]).astype(BF)
@@ -207,18 +288,18 @@
     loads[5].wait()
     dattend = dot(g2[core], wo[...], NT).astype(BF)
     stage_pairs(st_qd, query, dattend)
-    peers(lambda peer: to_whole(1, st_qd, qd_w, peer).start())
+    for off in range(1, N_PATCH):
+        to_whole(1, st_qd, qd_w, turn(off, -1)).start()
     qd_w[me] = st_qd[me]
-    peers(lambda peer: to_quarter(0, st_kv, kv_q, peer).start())
-    kv_q[me] = st_kv[N_PATCH + mine_e]
+    send_quarter(0, st_kv, kv_q)
     for e in range(2):
-        peer, copy = quarter_rows(e)
-
-        @pl.when(peer != me)
+        here, copy = quarter_rows(e)
+
+        @pl.when(jnp.logical_not(here))
         def _():
             copy.start()
 
-        @pl.when(peer == me)
+        @pl.when(here)
         def _():
             qd_q[lax.rem(me, 2)] = st_qd[N_PATCH + e]
 
@@ -235,7 +316,6 @@
     value_old = dot(s[...], wv[...]).astype(BF)
     stage_pairs(st_ks, key_old, value_old)
     ks_w[me] = st_ks[me]
-    ks_q[me] = st_ks[N_PATCH + mine_e]
 
     @pl.when(core == 0)
     def _():
@@ -262,19 +342,19 @@
         )
 
     def go_home_rows(kind, src, land, t):
-        peer = first_q + t
-        return peer, pltpu.make_async_remote_copy(
+        return pltpu.make_async_remote_copy(
             src_ref=src.at[t], dst_ref=land.at[N_PATCH + mine_e],
             send_sem=psend.at[kind, t], recv_sem=precv.at[kind, mine_e],
-            device_id=(img, peer), device_id_type=MESH,
+            device_id=(shared_img, first_q + t), device_id_type=MESH,
         )
 
     def come_home_rows(kind, land, e):
-        peer = 4 * e + me // 2
-        return peer, pltpu.make_async_remote_copy(
+        there, peer = helper(core, e)
+        here = jnp.logical_and(there == img, peer == me)
+        return here, pltpu.make_async_remote_copy(
             src_ref=land.at[N_PATCH + e], dst_ref=land.at[N_PATCH + e],
             send_sem=psend.at[kind, e], recv_sem=precv.at[kind, e],
-            device_id=(img, peer), device_id_type=MESH,
+            device_id=(there, peer), device_id_type=MESH,
         )
 
     def a_home(i):
@@ -293,8 +373,8 @@
 
     def a_home_rows(t):
         return pltpu.make_async_remote_copy(
-            src_ref=row_a.at[t], dst_ref=home_a.at[core, N_PATCH + mine_e],
-            send_sem=apsend.at[t], recv_sem=aprecv.at[core, mine_e],
+            src_ref=row_a.at[t], dst_ref=home_a.at[shared_core, N_PATCH + mine_e],
+            send_sem=apsend.at[t], recv_sem=aprecv.at[shared_core, mine_e],
             device_id=(core_one, first_q + t), device_id_type=MESH,
         )
 
@@ -302,7 +382,7 @@
         return pltpu.make_async_remote_copy(
             src_ref=home_a.at[c, N_PATCH + e], dst_ref=home_a.at[c, N_PATCH + e],
             send_sem=apsend.at[e], recv_sem=aprecv.at[c, e],
-            device_id=(core_one, 4 * e + me // 2), device_id_type=MESH,
+            device_id=helper(c, e), device_id_type=MESH,
         )
 
     def stays(peer):
@@ -316,10 +396,19 @@
         acc[...] = jnp.zeros_like(acc)
 
     peers(lambda peer: from_whole(0, kv_w, peer).wait_recv())
-    peers(lambda peer: from_whole(1, qd_w, peer).wait_recv())
     clear()
 
-    def first_whole(i):
+    def first_whole(off):
+        i = turn(off)
+
+        @pl.when(off == 6)
+        def _():
+            pass_keys(0, 0, kv_q)
+
+        @pl.when(i != me)
+        def _():
+            from_whole(1, qd_w, i).wait_recv()
+
         e_w[i], out_a[i], stats[i], q_scaled[i] = fresh_first(
             qd_w[i], kv_w[...].reshape(TOKENS, 128), acc
         )
@@ -339,13 +428,11 @@
     home_dv[me] = out_dv[me]
     peers(lambda peer: to_whole(2, st_ks, ks_w, peer).start())
 
-    peers(lambda peer: from_quarter(0, kv_q, peer).wait_recv())
+    wait_keys(0, kv_q)
     for t in range(2):
-        peer, copy = quarter_rows_in(t)
-
-        @pl.when(peer != me)
-        def _():
-            copy.wait_recv()
+        @pl.when(jnp.logical_not(owned(t)))
+        def _():
+            quarter_rows_in(t).wait_recv()
 
     clear()
 
@@ -364,29 +451,12 @@
 
         @pl.when(here)
         def _():
-            home_a[1, N_PATCH + mine_e] = row_a[t]
+            home_a[shared_core, N_PATCH + mine_e] = row_a[t]
 
     put(part_dv)
-    peers(lambda peer: go_home(5, part_dv, home_dvp, peer).start())
-    home_dvp[me] = part_dv[me]
-    peers(lambda peer: to_quarter(2, st_ks, ks_q, peer).start())
-
-    clear()
-
-    def second_whole(i):
-        out_dq[i] = fresh_second(
-            qd_w[i], kv_w[...].reshape(TOKENS, 128), e_w[i], stats[i], q_scaled[i], acc
-        )
-
-        @pl.when(i != me)
-        def _():
-            go_home(0, out_dq, home_dq, i).start()
-
-    loop(0, N_PATCH, second_whole)
-    home_dq[me] = out_dq[me]
-    put(out_dk)
-    peers(lambda peer: go_home(1, out_dk, home_dk, peer).start())
-    home_dk[me] = out_dk[me]
+    pass_sums(2, part_dv, sib_dv)
+    send_sums(2, 5, part_dv, sib_dv, home_dvp)
+    send_quarter(2, st_ks, ks_q)
 
     def unfold(src, r):
         cols = slice(r * HEAD_DIM, (r + 1) * HEAD_DIM)
@@ -394,24 +464,23 @@
 
     def add_shared(land, parts):
         for e in range(2):
-            total = parts[4 * e].astype(F32)
-            for n in range(1, 4):
-                total = total + parts[4 * e + n].astype(F32)
+            first = 4 * e + 2 * core
+            total = parts[first].astype(F32) + parts[first + 1].astype(F32)
             land[N_PATCH + e] = total.astype(BF)
 
-    peers(lambda peer: come_home(3, home_dv, peer).wait_recv())
-    peers(lambda peer: come_home(5, home_dvp, peer).wait_recv())
-    add_shared(home_dv, home_dvp)
-    for r in range(2):
-        dv2[core, r * ROWS // 2 : (r + 1) * ROWS // 2] = unfold(home_dv, r)
-    dv_share = pltpu.make_async_remote_copy(
-        src_ref=dv2.at[1], dst_ref=dv2.at[1], send_sem=dsem.at[0], recv_sem=dsem.at[1],
-        device_id=(sibling, me), device_id_type=MESH,
-    )
+    def y_copy(off):
+        peer = lax.rem(yy + off, 4)
+        return pltpu.make_async_remote_copy(
+            src_ref=grads.at[:, pl.ds(pl.multiple_of(SLOT * peer, 16), SLOT)],
+            dst_ref=from_y.at[off - 1],
+            send_sem=ysend.at[off - 1], recv_sem=yrecv.at[off - 1],
+            device_id=(4 * peer + 2 * zlo + core, me), device_id_type=MESH,
+        )
+
+    grads[:, 800:] = jnp.zeros((N_PATCH, PART - 800, 128), BF)
 
     @pl.when(core == 1)
     def _():
-        dv_share.start()
         for c in range(2):
             for n in range(N_PATCH):
                 if c == 1:
@@ -421,11 +490,10 @@
                 else:
                     a_in(c, n).wait_recv()
             for e in range(2):
-                if c == 1:
-                    @pl.when(4 * e + me // 2 != me)
-                    def _():
-                        a_in_rows(c, e).wait_recv()
-                else:
+                there, peer = helper(c, e)
+
+                @pl.when(jnp.logical_not(jnp.logical_and(there == img, peer == me)))
+                def _():
                     a_in_rows(c, e).wait_recv()
         a_t = jnp.concatenate(
             [unfold(home_a.at[c], r).T for c in range(2) for r in range(2)], axis=1
@@ -435,6 +503,36 @@
             part = dot(a_t[80 * q : 80 * q + 80], g_all).astype(BF)
             for c in range(10):
                 grads[q, 80 * c : 80 * c + 80] = part[:, 128 * c : 128 * c + 128]
+        for off in range(1, 4):
+            y_copy(off).start()
+
+    clear()
+
+    def second_whole(off):
+        i = turn(off)
+        out_dq[i] = fresh_second(
+            qd_w[i], kv_w[...].reshape(TOKENS, 128), e_w[i], stats[i], q_scaled[i], acc
+        )
+
+        @pl.when(i != me)
+        def _():
+            go_home(0, out_dq, home_dq, i).start()
+
+    loop(0, N_PATCH // 2, second_whole)
+
+    peers(lambda peer: come_home(3, home_dv, peer).wait_recv())
+    receive_sums(5, home_dvp)
+    add_shared(home_dv, home_dvp)
+    for r in range(2):
+        dv2[core, r * ROWS // 2 : (r + 1) * ROWS // 2] = unfold(home_dv, r)
+    dv_share = pltpu.make_async_remote_copy(
+        src_ref=dv2.at[1], dst_ref=dv2.at[1], send_sem=dsem.at[0], recv_sem=dsem.at[1],
+        device_id=(sibling, me), device_id_type=MESH,
+    )
+
+    @pl.when(core == 1)
+    def _():
+        dv_share.start()
 
     @pl.when(core == 0)
     def _():
@@ -444,20 +542,14 @@
             part = dot(x_t[160 * q : 160 * q + 160], dv_all).astype(BF)
             for c in range(5):
                 grads[q, 160 * c : 160 * c + 160] = part[:, 128 * c : 128 * c + 128]
-
-    grads[:, 800:] = jnp.zeros((N_PATCH, PART - 800, 128), BF)
-
-    def y_copy(off):
-        peer = lax.rem(yy + off, 4)
-        return pltpu.make_async_remote_copy(
-            src_ref=grads.at[:, pl.ds(pl.multiple_of(SLOT * peer, 16), SLOT)],
-            dst_ref=from_y.at[off - 1],
-            send_sem=ysend.at[off - 1], recv_sem=yrecv.at[off - 1],
-            device_id=(4 * peer + 2 * zlo + core, me), device_id_type=MESH,
-        )
-
-    for off in range(1, 4):
-        y_copy(off).start()
+        for off in range(1, 4):
+            y_copy(off).start()
+
+    loop(N_PATCH // 2, N_PATCH, second_whole)
+    home_dq[me] = out_dq[me]
+    put(out_dk)
+    peers(lambda peer: go_home(1, out_dk, home_dk, peer).start())
+    home_dk[me] = out_dk[me]
 
     clear()
 
@@ -471,25 +563,32 @@
 
     def send_rows(kind, src, land):
         for t in range(2):
-            peer, copy = go_home_rows(kind, src, land, t)
-
-            @pl.when(peer != me)
+            @pl.when(jnp.logical_not(owned(t)))
             def _():
-                copy.start()
-
-            @pl.when(peer == me)
+                go_home_rows(kind, src, land, t).start()
+
+            @pl.when(owned(t))
             def _():
                 land[N_PATCH + mine_e] = src[t]
 
     send_rows(0, row_dq, home_dq)
     put(part_dk)
-    peers(lambda peer: go_home(4, part_dk, home_dkp, peer).start())
-    home_dkp[me] = part_dk[me]
+    pass_sums(3, part_dk, sib_dk)
 
     peers(lambda peer: from_whole(2, ks_w, peer).wait_recv())
     kmix[...] = ks_w[...]
 
-    def stale_whole(i):
+    def stale_whole(off):
+        i = turn(off)
+
+        @pl.when(off == 2)
+        def _():
+            send_sums(3, 4, part_dk, sib_dk, home_dkp)
+
+        @pl.when(off == 6)
+        def _():
+            pass_keys(1, 2, ks_q)
+
         kmix[i] = kv_w[i]
         out_t[i] = stale_tile(qd_w[i], kmix[...].reshape(TOKENS, 128))
         kmix[i] = ks_w[i]
@@ -500,7 +599,7 @@
 
     loop(0, N_PATCH, stale_whole)
     home_t[me] = out_t[me]
-    peers(lambda peer: from_quarter(2, ks_q, peer).wait_recv())
+    wait_keys(1, ks_q)
     kmix[...] = ks_q[...]
 
     def stale_quarter(t):
@@ -551,16 +650,16 @@
 
     def receive_rows(kind, land):
         for e in range(2):
-            peer, copy = come_home_rows(kind, land, e)
-
-            @pl.when(peer != me)
+            here, copy = come_home_rows(kind, land, e)
+
+            @pl.when(jnp.logical_not(here))
             def _():
                 copy.wait_recv()
 
     peers(lambda peer: come_home(0, home_dq, peer).wait_recv())
     receive_rows(0, home_dq)
     peers(lambda peer: come_home(1, home_dk, peer).wait_recv())
-    peers(lambda peer: come_home(4, home_dkp, peer).wait_recv())
+    receive_sums(4, home_dkp)
     add_shared(home_dk, home_dkp)
     dquery = jnp.concatenate([unfold(home_dq, 0), unfold(home_dq, 1)], axis=0)
     dkey = jnp.concatenate([unfold(home_dk, 0), unfold(home_dk, 1)], axis=0)
@@ -620,13 +719,33 @@
     for kind, stage, land in ((0, st_kv, kv_w), (1, st_qd, qd_w), (2, st_ks, ks_w)):
         peers(lambda peer: to_whole(kind, stage, land, peer).wait_send())
     for kind, stage, land in ((0, st_kv, kv_q), (2, st_ks, ks_q)):
-        peers(lambda peer: to_quarter(kind, stage, land, peer).wait_send())
+        def sent(e, n):
+            peer, copy = to_quarter(kind, stage, land, e, n)
+
+            @pl.when(peer != me)
+            def _():
+                copy.wait_send()
+
+        each_quarter(sent)
+
     for e in range(2):
-        peer, copy = quarter_rows(e)
-
-        @pl.when(peer != me)
+        here, copy = quarter_rows(e)
+
+        @pl.when(jnp.logical_not(here))
         def _():
             copy.wait_send()
+
+    @pl.when(holds)
+    def _():
+        hand_over(0, kv_q, kv_q).wait_send()
+        hand_over(1, ks_q, ks_q).wait_send()
+        peers(lambda peer: go_home(4, part_dk, home_dkp, peer).wait_send())
+        peers(lambda peer: go_home(5, part_dv, home_dvp, peer).wait_send())
+
+    @pl.when(jnp.logical_not(holds))
+    def _():
+        hand_over(2, part_dv, sib_dv).wait_send()
+        hand_over(3, part_dk, sib_dk).wait_send()
 
     @pl.when(core == 1)
     def _():
@@ -639,16 +758,14 @@
 
     for kind, src, land in (
         (0, out_dq, home_dq), (1, out_dk, home_dk), (2, out_t, home_t),
-        (3, out_dv, home_dv), (4, part_dk, home_dkp), (5, part_dv, home_dvp),
+        (3, out_dv, home_dv),
     ):
         peers(lambda peer: go_home(kind, src, land, peer).wait_send())
     for kind, src, land in ((0, row_dq, home_dq), (1, row_t, home_t)):
         for t in range(2):
-            peer, copy = go_home_rows(kind, src, land, t)
-
-            @pl.when(peer != me)
+            @pl.when(jnp.logical_not(owned(t)))
             def _():
-                copy.wait_send()
+                go_home_rows(kind, src, land, t).wait_send()
 
     for n in range(N_PATCH):
         @pl.when(jnp.logical_not(stays(n)))
@@ -716,7 +833,7 @@
             vm(8, half, 128), vm(8, half, 128), vm(8, half, 128), vm(8, half, 128), vm(8, half, 128),
             vm(8, half, 128), vm(8, half, 128), vm(2, half, 128), vm(2, half, 128), vm(2, half, 128),
             vm(2, 10, half, 128), vm(10, half, 128), vm(10, half, 128), vm(10, half, 128), vm(10, half, 128),
-            vm(8, half, 128), vm(8, half, 128),
+            vm(8, half, 128), vm(8, half, 128), vm(8, half, 128), vm(8, half, 128), dma(4), dma(4),
             dma(6, 8), dma(6, 8), dma(2, 2), dma(2, 2), dma(8), dma(2, 8), dma(2), dma(2, 2),
             vm(C, 2 * ROWS), vm(2, ROWS, INNER), vm(8, PART, 128), vm(3, 8, SLOT, 128), vm(8, 2 * HALF, 128),
             vm(16, HALF, 128), vm(16, HALF, 128), vm(2, PART, 128, dtype=F32),
@@ -734,7 +851,7 @@
         in_specs=[anywhere] * 4,
         out_specs=[anywhere] * 4,
         scratch_shapes=[pltpu.VMEM(shape.shape, shape.dtype) for shape in shapes] + [dma(4), dma(4)],
-        compiler_params=pltpu.CompilerParams(vmem_limit_bytes=16 * 2**20),
+        compiler_params=pltpu.CompilerParams(vmem_limit_bytes=56 * 2**20),
         cost_estimate=pl.CostEstimate(flops=0, bytes_accessed=2 * 2**20, transcendentals=0),
     )(*results)
 

time: 104 us -> 91.7 us (0.88); the launches traced: 104 us -> 90.6 us
  Pallas kernels: 99.2 us -> 89.8 us
  local copies, waits for them, and re-layouts: 4.17 us -> 0 us
    pallas_call x1, Pallas kernels: 97 us -> 87.4 us  [on_device(): pl.pallas_call(kernel, out_shape=shapes, in_specs=[anywhere] * 7, out_spe...]
    unnamed x8 -> x0, local copies, waits for them, and re-layouts: 4.17 us -> none
where the time goes in v3:
time: 91.7 us; the launch traced here: 90.6 us
  Pallas kernels  89.8 us (98%)
    pallas_call x1, Pallas kernels, on_device(): pl.pallas_call(kernel, out_shape=shapes, in_specs=[anywhere] * 7, out_spe...  87.4 us
    pallas_call x1, Pallas kernels, on_device(): pl.pallas_call(pass_on, out_shape=shapes, in_specs=[anywhere] * 4, out_sp...  2.48 us

profile of v3, /device:TPU:1, one launch (start us, length us, event | category | flops | bytes accessed | tf_op | source)
XLA Modules:
  0.0 90.6 jit_solution(8285648001932632787)
XLA Ops:
  0.6 87.4 %shard_map.102 = (bf16[1,256,1280]{2,1,0:T(8,128)(2,1)}, bf16[1,256,1280]{2,1,0:T(8,128)(2,1)}, f32[160,640]{1,0:T(8,128)}, f32[80,1280]{1,0:T(8,128)}) custom-call(bf16[256,1280]{1,0:T(8,128)(2,1)} %bitcast.3, bf16[256,1280]{1,0:T(8,128)(2,1)} %bitcast.4, bf16[1280,640]{1,0:T(8,128)(2,1)} %wq_hbm.1, bf16[1280,640]{1,0:T(8,128)(2,1)} %wk_hbm.1, ...), custom_call_target="tpu_custom_call" | custom-call | flops 10000000000 | bytes 12582912 | tf_op jit(solution)/shard_map/pallas_call | solution.py:819
  88.0 2.5 %shard_map.103 = (bf16[1,256,1280]{2,1,0:T(8,128)(2,1)}, bf16[1,256,1280]{2,1,0:T(8,128)(2,1)}, f32[160,640]{1,0:T(8,128)}, f32[80,1280]{1,0:T(8,128)}) custom-call(bf16[1,256,1280]{2,1,0:T(8,128)(2,1)} %get-tuple-element.8.refs_0_, bf16[1,256,1280]{2,1,0:T(8,128)(2,1)} %get-tuple-element.9.refs_1_, f32[160,640]{1,0:T(8,128)} %get-tuple-element.10.refs_2_, ...), custom_call_target="tpu_custom_call" | custom-call | bytes 2097152 | tf_op jit(solution)/shard_map/pallas_call | solution.py:848

commit v4 on v3

--- a/solution.py
+++ b/solution.py
@@ -51,25 +51,37 @@
     return e.astype(BF), inv
 
 
-def fresh_first(qd, kv, acc):
+def both(parts, axis):
+    return jnp.concatenate(parts, axis=axis)
+
+
+def fresh_first(blocks, kv, acc):
     left = left_half(ROWS)
-    e16, inv = probabilities(qd, kv)
-    a16 = (dot(e16, kv) * inv).astype(BF)
-    delta = jnp.sum(
-        jnp.where(left, 0.0, a16.astype(F32) * qd.astype(F32)), axis=1, keepdims=True
-    )
-    scaled = (qd.astype(F32) * jnp.where(left, inv * SCALE, inv)).T.astype(BF)
-    acc[...] += dot(scaled[HEAD_DIM:], e16)
-    return e16, fold(a16, HEAD_DIM), jnp.where(left, inv * SCALE, delta), scaled[:HEAD_DIM]
-
-
-def fresh_second(qd, kv, e16, stats, q_scaled, acc):
+    outs, terms, rows = [], [], []
+    for qd in blocks:
+        e16, inv = probabilities(qd, kv)
+        a16 = (dot(e16, kv) * inv).astype(BF)
+        delta = jnp.sum(
+            jnp.where(left, 0.0, a16.astype(F32) * qd.astype(F32)), axis=1, keepdims=True
+        )
+        scaled = (qd.astype(F32) * jnp.where(left, inv * SCALE, inv)).T.astype(BF)
+        outs.append((e16, fold(a16, HEAD_DIM), jnp.where(left, inv * SCALE, delta), scaled[:HEAD_DIM]))
+        terms.append(e16)
+        rows.append(scaled[HEAD_DIM:])
+    acc[...] += dot(both(rows, 1), both(terms, 0))
+    return outs
+
+
+def fresh_second(blocks, kv, es, stats, q_scaled, acc):
     left = left_half(ROWS)
-    dprob = dot(jnp.where(left, jnp.zeros_like(qd), qd), kv, NT)
-    ds = (e16.astype(F32) * (dprob - stats[:, HEAD_DIM : HEAD_DIM + 1])).astype(BF)
-    dq = dot(ds, kv) * stats[:, 0:1]
-    acc[...] += dot(q_scaled, ds)
-    return fold(dq.astype(BF), 0)
+    outs, terms = [], []
+    for qd, e16, row in zip(blocks, es, stats):
+        dprob = dot(jnp.where(left, jnp.zeros_like(qd), qd), kv, NT)
+        ds = (e16.astype(F32) * (dprob - row[:, HEAD_DIM : HEAD_DIM + 1])).astype(BF)
+        outs.append(fold((dot(ds, kv) * row[:, 0:1]).astype(BF), 0))
+        terms.append(ds)
+    acc[...] += dot(both(q_scaled, 1), both(terms, 0))
+    return outs
 
 
 def stale_tile(qd, kv):
@@ -398,26 +410,33 @@
     peers(lambda peer: from_whole(0, kv_w, peer).wait_recv())
     clear()
 
-    def first_whole(off):
-        i = turn(off)
-
-        @pl.when(off == 6)
+    def first_pair(i, qd, kv, e, a):
+        outs = fresh_first([qd[n] for n in i[0]], kv[...].reshape(TOKENS, 128), acc)
+        for n, at, out in zip(*i, outs):
+            e[n], a[n], stats[at], q_scaled[at] = out
+
+    def two(k):
+        return turn(2 * k), turn(2 * k + 1)
+
+    def first_whole(k):
+        i = two(k)
+
+        @pl.when(k == 3)
         def _():
             pass_keys(0, 0, kv_q)
 
-        @pl.when(i != me)
-        def _():
-            from_whole(1, qd_w, i).wait_recv()
-
-        e_w[i], out_a[i], stats[i], q_scaled[i] = fresh_first(
-            qd_w[i], kv_w[...].reshape(TOKENS, 128), acc
-        )
-
-        @pl.when(jnp.logical_not(stays(i)))
-        def _():
-            a_home(i).start()
-
-    loop(0, N_PATCH, first_whole)
+        for n in i:
+            @pl.when(n != me)
+            def _():
+                from_whole(1, qd_w, n).wait_recv()
+
+        first_pair((i, i), qd_w, kv_w, e_w, out_a)
+        for n in i:
+            @pl.when(jnp.logical_not(stays(n)))
+            def _():
+                a_home(n).start()
+
+    loop(0, 4, first_whole)
 
     @pl.when(core == 1)
     def _():
@@ -436,12 +455,7 @@
 
     clear()
 
-    def first_quarter(t):
-        e_q[t], row_a[t], stats[N_PATCH + t], q_scaled[N_PATCH + t] = fresh_first(
-            qd_q[t], kv_q[...].reshape(TOKENS, 128), acc
-        )
-
-    loop(0, 2, first_quarter)
+    first_pair(((0, 1), (N_PATCH, N_PATCH + 1)), qd_q, kv_q, e_q, row_a)
     for t in range(2):
         here = stays(first_q + t)
 
@@ -479,73 +493,89 @@
 
     grads[:, 800:] = jnp.zeros((N_PATCH, PART - 800, 128), BF)
 
-    @pl.when(core == 1)
-    def _():
-        for c in range(2):
-            for n in range(N_PATCH):
-                if c == 1:
-                    @pl.when(n != me)
+    def make_grad_out():
+        @pl.when(core == 1)
+        def _():
+            for c in range(2):
+                for n in range(N_PATCH):
+                    if c == 1:
+                        @pl.when(n != me)
+                        def _():
+                            a_in(c, n).wait_recv()
+                    else:
+                        a_in(c, n).wait_recv()
+                for e in range(2):
+                    there, peer = helper(c, e)
+
+                    @pl.when(jnp.logical_not(jnp.logical_and(there == img, peer == me)))
                     def _():
-                        a_in(c, n).wait_recv()
-                else:
-                    a_in(c, n).wait_recv()
-            for e in range(2):
-                there, peer = helper(c, e)
-
-                @pl.when(jnp.logical_not(jnp.logical_and(there == img, peer == me)))
-                def _():
-                    a_in_rows(c, e).wait_recv()
-        a_t = jnp.concatenate(
-            [unfold(home_a.at[c], r).T for c in range(2) for r in range(2)], axis=1
-        )
-        g_all = g2[...].reshape(2 * ROWS, C)
-        for q in range(N_PATCH):
-            part = dot(a_t[80 * q : 80 * q + 80], g_all).astype(BF)
-            for c in range(10):
-                grads[q, 80 * c : 80 * c + 80] = part[:, 128 * c : 128 * c + 128]
-        for off in range(1, 4):
-            y_copy(off).start()
-
-    clear()
-
-    def second_whole(off):
-        i = turn(off)
-        out_dq[i] = fresh_second(
-            qd_w[i], kv_w[...].reshape(TOKENS, 128), e_w[i], stats[i], q_scaled[i], acc
-        )
-
-        @pl.when(i != me)
-        def _():
-            go_home(0, out_dq, home_dq, i).start()
-
-    loop(0, N_PATCH // 2, second_whole)
-
-    peers(lambda peer: come_home(3, home_dv, peer).wait_recv())
-    receive_sums(5, home_dvp)
-    add_shared(home_dv, home_dvp)
-    for r in range(2):
-        dv2[core, r * ROWS // 2 : (r + 1) * ROWS // 2] = unfold(home_dv, r)
+                        a_in_rows(c, e).wait_recv()
+            a_t = jnp.concatenate(
+                [unfold(home_a.at[c], r).T for c in range(2) for r in range(2)], axis=1
+            )
+            g_all = g2[...].reshape(2 * ROWS, C)
+            for q in range(N_PATCH):
+                part = dot(a_t[80 * q : 80 * q + 80], g_all).astype(BF)
+                for c in range(10):
+                    grads[q, 80 * c : 80 * c + 80] = part[:, 128 * c : 128 * c + 128]
+            for off in range(1, 4):
+                y_copy(off).start()
+
     dv_share = pltpu.make_async_remote_copy(
         src_ref=dv2.at[1], dst_ref=dv2.at[1], send_sem=dsem.at[0], recv_sem=dsem.at[1],
         device_id=(sibling, me), device_id_type=MESH,
     )
 
-    @pl.when(core == 1)
-    def _():
-        dv_share.start()
-
-    @pl.when(core == 0)
-    def _():
-        dv_share.wait_recv()
-        dv_all = dv2[...].reshape(2 * ROWS, INNER)
-        for q in range(N_PATCH):
-            part = dot(x_t[160 * q : 160 * q + 160], dv_all).astype(BF)
-            for c in range(5):
-                grads[q, 160 * c : 160 * c + 160] = part[:, 128 * c : 128 * c + 128]
-        for off in range(1, 4):
-            y_copy(off).start()
-
-    loop(N_PATCH // 2, N_PATCH, second_whole)
+    def make_grad_value():
+
+        peers(lambda peer: come_home(3, home_dv, peer).wait_recv())
+        receive_sums(5, home_dvp)
+        add_shared(home_dv, home_dvp)
+        for r in range(2):
+            dv2[core, r * ROWS // 2 : (r + 1) * ROWS // 2] = unfold(home_dv, r)
+        @pl.when(core == 1)
+        def _():
+            dv_share.start()
+
+        @pl.when(core == 0)
+        def _():
+            dv_share.wait_recv()
+            dv_all = dv2[...].reshape(2 * ROWS, INNER)
+            for q in range(N_PATCH):
+                part = dot(x_t[160 * q : 160 * q + 160], dv_all).astype(BF)
+                for c in range(5):
+                    grads[q, 160 * c : 160 * c + 160] = part[:, 128 * c : 128 * c + 128]
+            for off in range(1, 4):
+                y_copy(off).start()
+
+    clear()
+
+    def second_pair(i, qd, kv, e, out):
+        dqs = fresh_second(
+            [qd[n] for n in i[0]], kv[...].reshape(TOKENS, 128), [e[n] for n in i[0]],
+            [stats[n] for n in i[1]], [q_scaled[n] for n in i[1]], acc,
+        )
+        for n, dq in zip(i[0], dqs):
+            out[n] = dq
+
+    def second_whole(k):
+        i = two(k)
+
+        @pl.when(k == 1)
+        def _():
+            make_grad_out()
+
+        @pl.when(k == 3)
+        def _():
+            make_grad_value()
+
+        second_pair((i, i), qd_w, kv_w, e_w, out_dq)
+        for n in i:
+            @pl.when(n != me)
+            def _():
+                go_home(0, out_dq, home_dq, n).start()
+
+    loop(0, 4, second_whole)
     home_dq[me] = out_dq[me]
     put(out_dk)
     peers(lambda peer: go_home(1, out_dk, home_dk, peer).start())
@@ -553,13 +583,7 @@
 
     clear()
 
-    def second_quarter(t):
-        row_dq[t] = fresh_second(
-            qd_q[t], kv_q[...].reshape(TOKENS, 128), e_q[t], stats[N_PATCH + t],
-            q_scaled[N_PATCH + t], acc,
-        )
-
-    loop(0, 2, second_quarter)
+    second_pair(((0, 1), (N_PATCH, N_PATCH + 1)), qd_q, kv_q, e_q, row_dq)
 
     def send_rows(kind, src, land):
         for t in range(2):
@@ -575,53 +599,6 @@
     put(part_dk)
     pass_sums(3, part_dk, sib_dk)
 
-    peers(lambda peer: from_whole(2, ks_w, peer).wait_recv())
-    kmix[...] = ks_w[...]
-
-    def stale_whole(off):
-        i = turn(off)
-
-        @pl.when(off == 2)
-        def _():
-            send_sums(3, 4, part_dk, sib_dk, home_dkp)
-
-        @pl.when(off == 6)
-        def _():
-            pass_keys(1, 2, ks_q)
-
-        kmix[i] = kv_w[i]
-        out_t[i] = stale_tile(qd_w[i], kmix[...].reshape(TOKENS, 128))
-        kmix[i] = ks_w[i]
-
-        @pl.when(i != me)
-        def _():
-            go_home(2, out_t, home_t, i).start()
-
-    loop(0, N_PATCH, stale_whole)
-    home_t[me] = out_t[me]
-    wait_keys(1, ks_q)
-    kmix[...] = ks_q[...]
-
-    def stale_quarter(t):
-        i = first_q + t
-        kmix[i] = kv_q[i]
-        row_t[t] = stale_tile(qd_q[t], kmix[...].reshape(TOKENS, 128))
-        kmix[i] = ks_q[i]
-
-    loop(0, 2, stale_quarter)
-    send_rows(1, row_t, home_t)
-
-    for off in range(1, 4):
-        y_copy(off).wait_recv()
-
-    def y_add(q):
-        total = grads[q, pl.ds(pl.multiple_of(SLOT * yy, 16), SLOT)].astype(F32)
-        for n in range(3):
-            total = total + from_y[n, q].astype(F32)
-        ysum[q, :SLOT] = total.astype(BF)
-        ysum[q, SLOT:] = jnp.zeros((2 * HALF - SLOT, 128), BF)
-
-    loop(0, N_PATCH, y_add)
     plane = zlo * N_PATCH + me
 
     def xz_peer(off):
@@ -645,8 +622,86 @@
             device_id=(4 * yy + 2 * z_there + core, p_there), device_id_type=MESH,
         )
 
-    loop(1, 16, lambda off: xz_send(off).start())
-    from_xz[plane] = ysum[me, pl.ds(pl.multiple_of(HALF * zlo, 16), HALF)]
+    def sum_over_y():
+        for off in range(1, 4):
+            y_copy(off).wait_recv()
+
+        def y_add(q):
+            total = grads[q, pl.ds(pl.multiple_of(SLOT * yy, 16), SLOT)].astype(F32)
+            for n in range(3):
+                total = total + from_y[n, q].astype(F32)
+            ysum[q, :SLOT] = total.astype(BF)
+            ysum[q, SLOT:] = jnp.zeros((2 * HALF - SLOT, 128), BF)
+
+        loop(0, N_PATCH, y_add)
+        loop(1, 16, lambda off: xz_send(off).start())
+        from_xz[plane] = ysum[me, pl.ds(pl.multiple_of(HALF * zlo, 16), HALF)]
+
+    peers(lambda peer: from_whole(2, ks_w, peer).wait_recv())
+    kmix[0] = ks_w[...]
+    kmix[1] = ks_w[...]
+
+    def stale_pair(at, i, qd, kv, ks, out):
+        for t in range(2):
+            kmix[t, i[t]] = kv[i[t]]
+        outs = [stale_tile(qd[at[t]], kmix[t].reshape(TOKENS, 128)) for t in range(2)]
+        for t in range(2):
+            out[at[t]] = outs[t]
+            kmix[t, i[t]] = ks[i[t]]
+
+    def stale_whole(k):
+        i = two(k)
+
+        @pl.when(k == 3)
+        def _():
+            sum_over_y()
+
+        @pl.when(k == 1)
+        def _():
+            send_sums(3, 4, part_dk, sib_dk, home_dkp)
+
+        @pl.when(k == 3)
+        def _():
+            pass_keys(1, 2, ks_q)
+
+        stale_pair(i, i, qd_w, kv_w, ks_w, out_t)
+        for n in i:
+            @pl.when(n != me)
+            def _():
+                go_home(2, out_t, home_t, n).start()
+
+    loop(0, 4, stale_whole)
+    home_t[me] = out_t[me]
+    wait_keys(1, ks_q)
+    kmix[0] = ks_q[...]
+    kmix[1] = ks_q[...]
+
+    stale_pair((0, 1), (first_q, first_q + 1), qd_q, kv_q, ks_q, row_t)
+    send_rows(1, row_t, home_t)
+
+    loop(1, 16, lambda off: xz_recv(off).wait_recv())
+    total = from_xz[0].astype(F32)
+    for n in range(1, 16):
+        total = total + from_xz[n].astype(F32)
+    gathered[img] = total.astype(BF)
+
+    def gather_send(off):
+        peer = lax.rem(img + off, N_IMG)
+        return pltpu.make_async_remote_copy(
+            src_ref=gathered.at[img], dst_ref=gathered.at[img],
+            send_sem=gsend.at[peer], recv_sem=grecv.at[img],
+            device_id=(peer, me), device_id_type=MESH,
+        )
+
+    def gather_recv(off):
+        peer = lax.rem(img + off, N_IMG)
+        return pltpu.make_async_remote_copy(
+            src_ref=gathered.at[peer], dst_ref=gathered.at[peer],
+            send_sem=gsend.at[peer], recv_sem=grecv.at[peer],
+            device_id=(peer, me), device_id_type=MESH,
+        )
+
+    loop(1, N_IMG, lambda off: gather_send(off).start())
 
     def receive_rows(kind, land):
         for e in range(2):
@@ -668,30 +723,6 @@
     ).astype(BF)
     gradx_copy = pltpu.make_async_copy(gradx, gradx_out.at[0], out_sem.at[0])
     gradx_copy.start()
-
-    loop(1, 16, lambda off: xz_recv(off).wait_recv())
-    total = from_xz[0].astype(F32)
-    for n in range(1, 16):
-        total = total + from_xz[n].astype(F32)
-    gathered[img] = total.astype(BF)
-
-    def gather_send(off):
-        peer = lax.rem(img + off, N_IMG)
-        return pltpu.make_async_remote_copy(
-            src_ref=gathered.at[img], dst_ref=gathered.at[img],
-            send_sem=gsend.at[peer], recv_sem=grecv.at[img],
-            device_id=(peer, me), device_id_type=MESH,
-        )
-
-    def gather_recv(off):
-        peer = lax.rem(img + off, N_IMG)
-        return pltpu.make_async_remote_copy(
-            src_ref=gathered.at[peer], dst_ref=gathered.at[peer],
-            send_sem=gsend.at[peer], recv_sem=grecv.at[peer],
-            device_id=(peer, me), device_id_type=MESH,
-        )
-
-    loop(1, N_IMG, lambda off: gather_send(off).start())
 
     peers(lambda peer: come_home(2, home_t, peer).wait_recv())
     receive_rows(1, home_t)
@@ -829,7 +860,7 @@
             vm(8, ROWS, 128), vm(2, ROWS, 128), vm(8, ROWS, 128),
             dma(3, 8), dma(3, 8), dma(3, 8), dma(3, 8),
             vm(8, ROWS, TOKENS), vm(2, ROWS, TOKENS), vm(10, ROWS, 128, dtype=F32), vm(10, HEAD_DIM, ROWS),
-            vm(HEAD_DIM, TOKENS, dtype=F32), vm(8, ROWS, 128),
+            vm(HEAD_DIM, TOKENS, dtype=F32), vm(2, 8, ROWS, 128),
             vm(8, half, 128), vm(8, half, 128), vm(8, half, 128), vm(8, half, 128), vm(8, half, 128),
             vm(8, half, 128), vm(8, half, 128), vm(2, half, 128), vm(2, half, 128), vm(2, half, 128),
             vm(2, 10, half, 128), vm(10, half, 128), vm(10, half, 128), vm(10, half, 128), vm(10, half, 128),

time: 91.7 us -> 86 us (0.938); the launches traced: 90.6 us -> 85.9 us
  Pallas kernels: 89.8 us -> 85.1 us
    pallas_call x1, Pallas kernels: 87.4 us -> 82.6 us  [on_device(): pl.pallas_call(kernel, out_shape=shapes, in_specs=[anywhere] * 7, out_spe...]
where the time goes in v4:
time: 86 us; the launch traced here: 85.9 us
  Pallas kernels  85.1 us (99%)
    pallas_call x1, Pallas kernels, on_device(): pl.pallas_call(kernel, out_shape=shapes, in_specs=[anywhere] * 7, out_spe...  82.6 us
    pallas_call x1, Pallas kernels, on_device(): pl.pallas_call(pass_on, out_shape=shapes, in_specs=[anywhere] * 4, out_sp...  2.48 us

profile of v4, /device:TPU:1, one launch (start us, length us, event | category | flops | bytes accessed | tf_op | source)
XLA Modules:
  0.0 85.9 jit_solution(12436860278511116286)
XLA Ops:
  0.6 82.6 %shard_map.102 = (bf16[1,256,1280]{2,1,0:T(8,128)(2,1)}, bf16[1,256,1280]{2,1,0:T(8,128)(2,1)}, f32[160,640]{1,0:T(8,128)}, f32[80,1280]{1,0:T(8,128)}) custom-call(bf16[256,1280]{1,0:T(8,128)(2,1)} %bitcast.3, bf16[256,1280]{1,0:T(8,128)(2,1)} %bitcast.4, bf16[1280,640]{1,0:T(8,128)(2,1)} %wq_hbm.1, bf16[1280,640]{1,0:T(8,128)(2,1)} %wk_hbm.1, ...), custom_call_target="tpu_custom_call" | custom-call | flops 10000000000 | bytes 12582912 | tf_op jit(solution)/shard_map/pallas_call | solution.py:850
  83.2 2.5 %shard_map.103 = (bf16[1,256,1280]{2,1,0:T(8,128)(2,1)}, bf16[1,256,1280]{2,1,0:T(8,128)(2,1)}, f32[160,640]{1,0:T(8,128)}, f32[80,1280]{1,0:T(8,128)}) custom-call(bf16[1,256,1280]{2,1,0:T(8,128)(2,1)} %get-tuple-element.8.refs_0_, bf16[1,256,1280]{2,1,0:T(8,128)(2,1)} %get-tuple-element.9.refs_1_, f32[160,640]{1,0:T(8,128)} %get-tuple-element.10.refs_2_, ...), custom_call_target="tpu_custom_call" | custom-call | bytes 2097152 | tf_op jit(solution)/shard_map/pallas_call | solution.py:879

commit v5 on v4

--- a/solution.py
+++ b/solution.py
@@ -445,7 +445,6 @@
     put(out_dv)
     peers(lambda peer: go_home(3, out_dv, home_dv, peer).start())
     home_dv[me] = out_dv[me]
-    peers(lambda peer: to_whole(2, st_ks, ks_w, peer).start())
 
     wait_keys(0, kv_q)
     for t in range(2):
@@ -470,6 +469,7 @@
     put(part_dv)
     pass_sums(2, part_dv, sib_dv)
     send_sums(2, 5, part_dv, sib_dv, home_dvp)
+    peers(lambda peer: to_whole(2, st_ks, ks_w, peer).start())
     send_quarter(2, st_ks, ks_q)
 
     def unfold(src, r):
@@ -565,7 +565,7 @@
         def _():
             make_grad_out()
 
-        @pl.when(k == 3)
+        @pl.when(k == 2)
         def _():
             make_grad_value()
 
@@ -652,7 +652,7 @@
     def stale_whole(k):
         i = two(k)
 
-        @pl.when(k == 3)
+        @pl.when(k == 4)
         def _():
             sum_over_y()
 
@@ -672,6 +672,7 @@
 
     loop(0, 4, stale_whole)
     home_t[me] = out_t[me]
+    sum_over_y()
     wait_keys(1, ks_q)
     kmix[0] = ks_q[...]
     kmix[1] = ks_q[...]

time: 86 us -> 82.7 us (0.962)
  Pallas kernels: 85.1 us -> 81.7 us
    pallas_call x1, Pallas kernels: 82.6 us -> 79.2 us  [on_device(): pl.pallas_call(kernel, out_shape=shapes, in_specs=[anywhere] * 7, out_spe...]
where the time goes in v5:
time: 82.7 us; the launch traced here: 82.5 us
  Pallas kernels  81.7 us (99%)
    pallas_call x1, Pallas kernels, on_device(): pl.pallas_call(kernel, out_shape=shapes, in_specs=[anywhere] * 7, out_spe...  79.2 us
    pallas_call x1, Pallas kernels, on_device(): pl.pallas_call(pass_on, out_shape=shapes, in_specs=[anywhere] * 4, out_sp...  2.48 us

profile of v5, /device:TPU:1, one launch (start us, length us, event | category | flops | bytes accessed | tf_op | source)
XLA Modules:
  0.0 82.5 jit_solution(5817389330755850610)
XLA Ops:
  0.6 79.2 %shard_map.102 = (bf16[1,256,1280]{2,1,0:T(8,128)(2,1)}, bf16[1,256,1280]{2,1,0:T(8,128)(2,1)}, f32[160,640]{1,0:T(8,128)}, f32[80,1280]{1,0:T(8,128)}) custom-call(bf16[256,1280]{1,0:T(8,128)(2,1)} %bitcast.3, bf16[256,1280]{1,0:T(8,128)(2,1)} %bitcast.4, bf16[1280,640]{1,0:T(8,128)(2,1)} %wq_hbm.1, bf16[1280,640]{1,0:T(8,128)(2,1)} %wk_hbm.1, ...), custom_call_target="tpu_custom_call" | custom-call | flops 10000000000 | bytes 12582912 | tf_op jit(solution)/shard_map/pallas_call | solution.py:851
  79.9 2.5 %shard_map.103 = (bf16[1,256,1280]{2,1,0:T(8,128)(2,1)}, bf16[1,256,1280]{2,1,0:T(8,128)(2,1)}, f32[160,640]{1,0:T(8,128)}, f32[80,1280]{1,0:T(8,128)}) custom-call(bf16[1,256,1280]{2,1,0:T(8,128)(2,1)} %get-tuple-element.8.refs_0_, bf16[1,256,1280]{2,1,0:T(8,128)(2,1)} %get-tuple-element.9.refs_1_, f32[160,640]{1,0:T(8,128)} %get-tuple-element.10.refs_2_, ...), custom_call_target="tpu_custom_call" | custom-call | bytes 2097152 | tf_op jit(solution)/shard_map/pallas_call | solution.py:880

commit v6 on v5

--- a/solution.py
+++ b/solution.py
@@ -626,15 +626,21 @@
         for off in range(1, 4):
             y_copy(off).wait_recv()
 
-        def y_add(q):
+        def y_add(k):
+            q = turn(k)
             total = grads[q, pl.ds(pl.multiple_of(SLOT * yy, 16), SLOT)].astype(F32)
             for n in range(3):
                 total = total + from_y[n, q].astype(F32)
             ysum[q, :SLOT] = total.astype(BF)
             ysum[q, SLOT:] = jnp.zeros((2 * HALF - SLOT, 128), BF)
+            for z_there in range(2):
+                there = z_there * N_PATCH + q
+
+                @pl.when(there != plane)
+                def _():
+                    xz_send(lax.rem(there + 16 - plane, 16)).start()
 
         loop(0, N_PATCH, y_add)
-        loop(1, 16, lambda off: xz_send(off).start())
         from_xz[plane] = ysum[me, pl.ds(pl.multiple_of(HALF * zlo, 16), HALF)]
 
     peers(lambda peer: from_whole(2, ks_w, peer).wait_recv())

time: 82.7 us -> 82 us (level)
  no operation moved by 1% of the time
where the time goes in v6:
time: 82 us; the launch traced here: 81.8 us
  Pallas kernels  81 us (99%)
    pallas_call x1, Pallas kernels, on_device(): pl.pallas_call(kernel, out_shape=shapes, in_specs=[anywhere] * 7, out_spe...  78.6 us
    pallas_call x1, Pallas kernels, on_device(): pl.pallas_call(pass_on, out_shape=shapes, in_specs=[anywhere] * 4, out_sp...  2.48 us

profile of v6, /device:TPU:1, one launch (start us, length us, event | category | flops | bytes accessed | tf_op | source)
XLA Modules:
  0.0 81.8 jit_solution(324114510454819738)
XLA Ops:
  0.6 78.6 %shard_map.102 = (bf16[1,256,1280]{2,1,0:T(8,128)(2,1)}, bf16[1,256,1280]{2,1,0:T(8,128)(2,1)}, f32[160,640]{1,0:T(8,128)}, f32[80,1280]{1,0:T(8,128)}) custom-call(bf16[256,1280]{1,0:T(8,128)(2,1)} %bitcast.3, bf16[256,1280]{1,0:T(8,128)(2,1)} %bitcast.4, bf16[1280,640]{1,0:T(8,128)(2,1)} %wq_hbm.1, bf16[1280,640]{1,0:T(8,128)(2,1)} %wk_hbm.1, ...), custom_call_target="tpu_custom_call" | custom-call | flops 10000000000 | bytes 12582912 | tf_op jit(solution)/shard_map/pallas_call | solution.py:857
  79.2 2.5 %shard_map.103 = (bf16[1,256,1280]{2,1,0:T(8,128)(2,1)}, bf16[1,256,1280]{2,1,0:T(8,128)(2,1)}, f32[160,640]{1,0:T(8,128)}, f32[80,1280]{1,0:T(8,128)}) custom-call(bf16[1,256,1280]{2,1,0:T(8,128)(2,1)} %get-tuple-element.8.refs_0_, bf16[1,256,1280]{2,1,0:T(8,128)(2,1)} %get-tuple-element.9.refs_1_, f32[160,640]{1,0:T(8,128)} %get-tuple-element.10.refs_2_, ...), custom_call_target="tpu_custom_call" | custom-call | bytes 2097152 | tf_op jit(solution)/shard_map/pallas_call | solution.py:886
